TPU v7x, 32 devices: a whole 2x2x4 slice. The times are simulated.
32 devices in a mesh: fsdp: 8 (over z, x), seq: 4 (over y, core).
Axes of the slice: x: 2, y: 2, z: 4, core: 2. Of those that a mesh axis runs over, the one named last changes fastest.
Arguments:
- tokens: bfloat16 [24, 1024, 1024], P('fsdp', 'seq'), may hold values from -6 to 6
- segments: int32 [24, 1024], P('fsdp', 'seq'), may hold values from 0 to 1023, as said below
- qkv_weight: bfloat16 [1024, 3072], P('fsdp'), may hold values from -0.1875 to 0.1875
- query_bias: bfloat16 [1024], P('fsdp'), may hold values from -3 to 3
- value_bias: bfloat16 [1024], P('fsdp'), may hold values from -3 to 3
- out_weight: bfloat16 [1024, 1024], P('fsdp'), may hold values from -1.5 to 1.5
- out_bias: bfloat16 [1024], P('fsdp'), may hold values from -3 to 3
- first_gain: bfloat16 [1024], P('fsdp'), may hold values from 0.5 to 1.5
- first_shift: bfloat16 [1024], P('fsdp'), may hold values from -3 to 3
- hidden_weight: bfloat16 [1024, 4096], P('fsdp'), may hold values from -0.1875 to 0.1875
- hidden_bias: bfloat16 [4096], P('fsdp'), may hold values from -3 to 3
- down_weight: bfloat16 [4096, 1024], P('fsdp'), may hold values from -0.09375 to 0.09375
- down_bias: bfloat16 [1024], P('fsdp'), may hold values from -3 to 3
- second_gain: bfloat16 [1024], P('fsdp'), may hold values from 0.5 to 1.5
- second_shift: bfloat16 [1024], P('fsdp'), may hold values from -3 to 3
- cotangent: bfloat16 [24, 1024, 1024], P('fsdp', 'seq'), may hold values from -6 to 6
Outputs:
- block_out: bfloat16 [24, 1024, 1024], P('fsdp', 'seq')
- grad_tokens: float32 [24, 1024, 1024], P('fsdp', 'seq')
- grad_qkv_weight: float32 [1024, 3072], P('fsdp')
- grad_query_bias: float32 [1024], P('fsdp')
- grad_value_bias: float32 [1024], P('fsdp')
- grad_out_weight: float32 [1024, 1024], P('fsdp')
- grad_out_bias: float32 [1024], P('fsdp')
- grad_first_gain: float32 [1024], P('fsdp')
- grad_first_shift: float32 [1024], P('fsdp')
- grad_hidden_weight: float32 [1024, 4096], P('fsdp')
- grad_hidden_bias: float32 [4096], P('fsdp')
- grad_down_weight: float32 [4096, 1024], P('fsdp')
- grad_down_bias: float32 [1024], P('fsdp')
- grad_second_gain: float32 [1024], P('fsdp')
- grad_second_shift: float32 [1024], P('fsdp')
Inputs may be any that keep to these rules, and one draw needn't show every extreme that they name: `segments`: A token's segment number is the position within its sequence of its document's first token, so it never falls along a sequence. On each index of fsdp one of its 3 sequences is a single document; every other sequence ends with a document of one token.
All inputs are finite; a program needn't handle non-finite values.
Results may differ from a plain program's by a relative error of at most 0.017.
Values may be sent and summed in bfloat16 or wider, within the bound.
A program may use at most 256 MiB of HBM per device.

v0:
```python
from functools import partial

import jax
import jax.numpy as jnp
from jax import lax
from jax.sharding import PartitionSpec as P

H = 16
DH = 64


norm_epsilon = 1e-05
masked_score = -1e30
heads_step = 2


def norm_rows(values, gain, shift):
    row_mean = jnp.mean(values, -1, keepdims=True)
    centered = values - row_mean
    inverse = lax.rsqrt(jnp.mean(centered * centered, -1, keepdims=True) + norm_epsilon)
    normed = centered * inverse
    return (normed * gain + shift, normed, inverse)


def norm_back(upstream, normed, inverse, gain):
    scaled = upstream * gain
    first_mean = jnp.mean(scaled, -1, keepdims=True)
    second_mean = jnp.mean(scaled * normed, -1, keepdims=True)
    result = inverse * (scaled - first_mean - normed * second_mean)
    return (result, jnp.sum(upstream * normed, axis=(0, 1)), jnp.sum(upstream, axis=(0, 1)))


def head_slice(array, head_index):
    group_width = heads_step * DH
    piece = lax.dynamic_slice_in_dim(array, head_index * group_width, group_width, 2)
    return piece.reshape(piece.shape[0], piece.shape[1], heads_step, DH)


def join_heads(stacked):
    return jnp.transpose(stacked, (1, 2, 0, 3)).reshape(stacked.shape[1], stacked.shape[2], -1)


def flat_heads(array):
    return array.reshape(array.shape[0], array.shape[1], heads_step * DH)


def group_scores(query_part, key_part, allowed):
    scores = jnp.einsum(
        "sqhe,skhe->shqk", query_part, key_part, preferred_element_type=jnp.float32
    ) * DH ** (-0.5)
    return jnp.where(allowed[:, None], scores, masked_score)


def attend_group(head_index, queries, key_rows, value_rows, allowed):
    query_part = head_slice(queries, head_index)
    key_part = head_slice(key_rows, head_index)
    value_part = head_slice(value_rows, head_index)
    scores = group_scores(query_part, key_part, allowed)
    row_peak = jnp.max(scores, -1, keepdims=True)
    shifted = jnp.exp(scores - row_peak)
    row_total = jnp.sum(shifted, -1, keepdims=True)
    weights_low = (shifted / row_total).astype(jnp.bfloat16)
    context = jnp.einsum(
        "shqk,skhe->sqhe", weights_low, value_part, preferred_element_type=jnp.float32
    )
    return (flat_heads(context), row_peak + jnp.log(row_total))


def score_grads(query_part, key_part, value_part, grad_part, allowed, log_total, row_inner):
    scores = group_scores(query_part, key_part, allowed)
    softmax_rows = jnp.exp(scores - log_total)
    grad_weights = jnp.einsum(
        "sqhe,skhe->shqk", grad_part, value_part, preferred_element_type=jnp.float32
    )
    row_inner = jnp.sum(softmax_rows * grad_weights, -1, keepdims=True)
    grad_scores = (softmax_rows * (grad_weights - row_inner)).astype(jnp.bfloat16)
    return (softmax_rows, grad_scores, row_inner)


def attend_back(head_index, log_total, queries, key_rows, value_rows, allowed, grad_context):
    query_part = head_slice(queries, head_index)
    key_part = head_slice(key_rows, head_index)
    value_part = head_slice(value_rows, head_index)
    grad_part = head_slice(grad_context, head_index)
    softmax_rows, grad_scores, row_inner = score_grads(
        query_part, key_part, value_part, grad_part, allowed, log_total, None
    )
    score_scale = DH ** (-0.5)
    grad_query = (
        jnp.einsum("shqk,skhe->sqhe", grad_scores, key_part, preferred_element_type=jnp.float32)
        * score_scale
    )
    grad_key = (
        jnp.einsum("shqk,sqhe->skhe", grad_scores, query_part, preferred_element_type=jnp.float32)
        * score_scale
    )
    grad_value = jnp.einsum(
        "shqk,sqhe->skhe",
        softmax_rows.astype(jnp.bfloat16),
        grad_part,
        preferred_element_type=jnp.float32,
    )
    return (flat_heads(grad_query), flat_heads(grad_key), flat_heads(grad_value), row_inner)


def body(
    tokens,
    segments,
    qkv_weight,
    query_bias,
    value_bias,
    out_weight,
    out_bias,
    first_gain,
    first_shift,
    hidden_weight,
    hidden_bias,
    down_weight,
    down_bias,
    second_gain,
    second_shift,
    cotangent,
):
    model_width = tokens.shape[2]
    qkv_full, qbias_full, vbias_full, out_full, obias_full, gain_one, shift_one = (
        lax.all_gather(qkv_weight, "fsdp", axis=0, tiled=True),
        lax.all_gather(query_bias, "fsdp", axis=0, tiled=True),
        lax.all_gather(value_bias, "fsdp", axis=0, tiled=True),
        lax.all_gather(out_weight, "fsdp", axis=0, tiled=True),
        lax.all_gather(out_bias, "fsdp", axis=0, tiled=True),
        lax.all_gather(first_gain, "fsdp", axis=0, tiled=True),
        lax.all_gather(first_shift, "fsdp", axis=0, tiled=True),
    )
    query_shift = qbias_full.astype(jnp.float32)
    value_shift = vbias_full.astype(jnp.float32)
    projected = jnp.dot(tokens, qkv_full, preferred_element_type=jnp.float32)
    queries = (projected[..., :model_width] + query_shift).astype(jnp.bfloat16)
    key_local = projected[..., model_width : 2 * model_width].astype(jnp.bfloat16)
    value_local = (projected[..., 2 * model_width :] + value_shift).astype(jnp.bfloat16)
    key_rows, value_rows, segment_all = (
        lax.all_gather(key_local, "seq", axis=1, tiled=True),
        lax.all_gather(value_local, "seq", axis=1, tiled=True),
        lax.all_gather(segments, "seq", axis=1, tiled=True),
    )
    allowed = segments[:, :, None] == segment_all[:, None, :]
    group_count = H // heads_step
    contexts, log_totals = lax.map(
        lambda head_index: attend_group(head_index, queries, key_rows, value_rows, allowed),
        jnp.arange(group_count),
    )
    context = join_heads(contexts).astype(jnp.bfloat16)
    attention = jnp.dot(context, out_full, preferred_element_type=jnp.float32) + obias_full.astype(
        jnp.float32
    )
    hidden, normed_one, inverse_one = norm_rows(
        tokens.astype(jnp.float32) + attention,
        gain_one.astype(jnp.float32),
        shift_one.astype(jnp.float32),
    )
    hidden_low = hidden.astype(jnp.bfloat16)
    up_full, upbias_full, down_full, downbias_full, gain_two, shift_two = (
        lax.all_gather(hidden_weight, "fsdp", axis=0, tiled=True),
        lax.all_gather(hidden_bias, "fsdp", axis=0, tiled=True),
        lax.all_gather(down_weight, "fsdp", axis=0, tiled=True),
        lax.all_gather(down_bias, "fsdp", axis=0, tiled=True),
        lax.all_gather(second_gain, "fsdp", axis=0, tiled=True),
        lax.all_gather(second_shift, "fsdp", axis=0, tiled=True),
    )
    preactivation = jnp.dot(
        hidden_low, up_full, preferred_element_type=jnp.float32
    ) + upbias_full.astype(jnp.float32)
    activation_low = jax.nn.gelu(preactivation, approximate=False).astype(jnp.bfloat16)
    branch = jnp.dot(
        activation_low, down_full, preferred_element_type=jnp.float32
    ) + downbias_full.astype(jnp.float32)
    output, normed_two, inverse_two = norm_rows(
        hidden + branch, gain_two.astype(jnp.float32), shift_two.astype(jnp.float32)
    )
    block_out = output.astype(jnp.bfloat16)
    up_back, down_back, gain_back_two = (
        lax.all_gather(hidden_weight, "fsdp", axis=0, tiled=True),
        lax.all_gather(down_weight, "fsdp", axis=0, tiled=True),
        lax.all_gather(second_gain, "fsdp", axis=0, tiled=True),
    )
    grad_two, grad_gain_two, grad_shift_two = norm_back(
        cotangent.astype(jnp.float32), normed_two, inverse_two, gain_back_two.astype(jnp.float32)
    )
    grad_branch = grad_two.astype(jnp.bfloat16)
    grad_down = jnp.einsum(
        "sbf,sbd->fd", activation_low, grad_branch, preferred_element_type=jnp.float32
    )
    grad_down_bias = jnp.sum(grad_branch.astype(jnp.float32), axis=(0, 1))
    grad_activation = jnp.einsum(
        "sbd,fd->sbf", grad_branch, down_back, preferred_element_type=jnp.float32
    )
    gelu_pull = jax.vjp(partial(jax.nn.gelu, approximate=False), preactivation)[1]
    grad_pre = gelu_pull(grad_activation)[0].astype(jnp.bfloat16)
    grad_up = jnp.einsum("sbd,sbf->df", hidden_low, grad_pre, preferred_element_type=jnp.float32)
    grad_up_bias = jnp.sum(grad_pre.astype(jnp.float32), axis=(0, 1))
    grad_hidden = grad_two + jnp.einsum(
        "sbf,df->sbd", grad_pre, up_back, preferred_element_type=jnp.float32
    )
    qkv_back, out_back, gain_back_one = (
        lax.all_gather(qkv_weight, "fsdp", axis=0, tiled=True),
        lax.all_gather(out_weight, "fsdp", axis=0, tiled=True),
        lax.all_gather(first_gain, "fsdp", axis=0, tiled=True),
    )
    grad_one, grad_gain_one, grad_shift_one = norm_back(
        grad_hidden, normed_one, inverse_one, gain_back_one.astype(jnp.float32)
    )
    grad_attention = grad_one.astype(jnp.bfloat16)
    grad_out = jnp.einsum(
        "sbc,sbd->cd", context, grad_attention, preferred_element_type=jnp.float32
    )
    grad_out_bias = jnp.sum(grad_attention.astype(jnp.float32), axis=(0, 1))
    grad_context = jnp.einsum(
        "sbd,cd->sbc", grad_attention, out_back, preferred_element_type=jnp.float32
    ).astype(jnp.bfloat16)
    grad_queries, grad_keys_all, grad_values_all, row_inners = lax.map(
        lambda scanned: attend_back(
            scanned[0], scanned[1], queries, key_rows, value_rows, allowed, grad_context
        ),
        (jnp.arange(group_count), log_totals),
    )
    grad_keys, grad_values = (
        lax.psum_scatter(
            join_heads(grad_keys_all).astype(jnp.bfloat16), "seq", scatter_dimension=1, tiled=True
        ).astype(jnp.float32),
        lax.psum_scatter(
            join_heads(grad_values_all).astype(jnp.bfloat16), "seq", scatter_dimension=1, tiled=True
        ).astype(jnp.float32),
    )
    grad_qkv_low = jnp.concatenate(
        [
            join_heads(grad_queries).astype(jnp.bfloat16),
            grad_keys.astype(jnp.bfloat16),
            grad_values.astype(jnp.bfloat16),
        ],
        axis=-1,
    )
    grad_qkv = jnp.einsum("sbd,sbe->de", tokens, grad_qkv_low, preferred_element_type=jnp.float32)
    grad_query_bias = jnp.sum(grad_qkv_low[..., :model_width].astype(jnp.float32), axis=(0, 1))
    grad_value_bias = jnp.sum(grad_qkv_low[..., 2 * model_width :].astype(jnp.float32), axis=(0, 1))
    grad_tokens = grad_one + jnp.einsum(
        "sbe,de->sbd", grad_qkv_low, qkv_back, preferred_element_type=jnp.float32
    )
    summed = (
        lax.psum_scatter(grad_qkv, "fsdp", scatter_dimension=0, tiled=True),
        lax.psum_scatter(grad_query_bias, "fsdp", scatter_dimension=0, tiled=True),
        lax.psum_scatter(grad_value_bias, "fsdp", scatter_dimension=0, tiled=True),
        lax.psum_scatter(grad_out, "fsdp", scatter_dimension=0, tiled=True),
        lax.psum_scatter(grad_out_bias, "fsdp", scatter_dimension=0, tiled=True),
        lax.psum_scatter(grad_gain_one, "fsdp", scatter_dimension=0, tiled=True),
        lax.psum_scatter(grad_shift_one, "fsdp", scatter_dimension=0, tiled=True),
        lax.psum_scatter(grad_up, "fsdp", scatter_dimension=0, tiled=True),
        lax.psum_scatter(grad_up_bias, "fsdp", scatter_dimension=0, tiled=True),
        lax.psum_scatter(grad_down, "fsdp", scatter_dimension=0, tiled=True),
        lax.psum_scatter(grad_down_bias, "fsdp", scatter_dimension=0, tiled=True),
        lax.psum_scatter(grad_gain_two, "fsdp", scatter_dimension=0, tiled=True),
        lax.psum_scatter(grad_shift_two, "fsdp", scatter_dimension=0, tiled=True),
    )
    summed = (
        lax.psum(summed[0].astype(jnp.bfloat16), "seq").astype(jnp.float32),
        lax.psum(summed[1].astype(jnp.bfloat16), "seq").astype(jnp.float32),
        lax.psum(summed[2].astype(jnp.bfloat16), "seq").astype(jnp.float32),
        lax.psum(summed[3].astype(jnp.bfloat16), "seq").astype(jnp.float32),
        lax.psum(summed[4].astype(jnp.bfloat16), "seq").astype(jnp.float32),
        lax.psum(summed[5].astype(jnp.bfloat16), "seq").astype(jnp.float32),
        lax.psum(summed[6].astype(jnp.bfloat16), "seq").astype(jnp.float32),
        lax.psum(summed[7].astype(jnp.bfloat16), "seq").astype(jnp.float32),
        lax.psum(summed[8].astype(jnp.bfloat16), "seq").astype(jnp.float32),
        lax.psum(summed[9].astype(jnp.bfloat16), "seq").astype(jnp.float32),
        lax.psum(summed[10].astype(jnp.bfloat16), "seq").astype(jnp.float32),
        lax.psum(summed[11].astype(jnp.bfloat16), "seq").astype(jnp.float32),
        lax.psum(summed[12].astype(jnp.bfloat16), "seq").astype(jnp.float32),
    )
    return (block_out, grad_tokens) + tuple(summed)


def solution(mesh):
    in_specs = (
        P("fsdp", "seq", None),
        P("fsdp", "seq"),
        P("fsdp", None),
        P("fsdp"),
        P("fsdp"),
        P("fsdp", None),
        P("fsdp"),
        P("fsdp"),
        P("fsdp"),
        P("fsdp", None),
        P("fsdp"),
        P("fsdp", None),
        P("fsdp"),
        P("fsdp"),
        P("fsdp"),
        P("fsdp", "seq", None),
    )
    out_specs = (
        P("fsdp", "seq", None),
        P("fsdp", "seq", None),
        P("fsdp", None),
        P("fsdp"),
        P("fsdp"),
        P("fsdp", None),
        P("fsdp"),
        P("fsdp"),
        P("fsdp"),
        P("fsdp", None),
        P("fsdp"),
        P("fsdp", None),
        P("fsdp"),
        P("fsdp"),
        P("fsdp"),
    )
    return jax.shard_map(body, mesh=mesh, in_specs=in_specs, out_specs=out_specs, check_vma=False)
```

profile of v0, /device:TPU:0, one launch (start us, length us, event | category | flops | bytes accessed | tf_op | source)
XLA Modules:
  0.0 1852.7 jit_solution(13842077172005202617)
XLA Ops:
  8.0 22.5 %all-gather = bf16[8,1,128]{2,1,0:T(2,128)(2,1)S(1)} all-gather(bf16[1,1,128]{2,1,0:T(2,128)(2,1)} %bitcast.236), channel_id=1, replica_groups=mesh['fsdp'=8,'seq'=4] {'fsdp'}, dimensions={0}, use_global_device_ids=true | all-gather | bytes 2304 | tf_op jit(solution)/shard_map/all_gather | solution.py:128
  30.5 16.7 all-gather.1
  47.1 64.9 %all-gather.16.cloned.1.call-done = bf16[1024,3072]{1,0:T(8,128)(2,1)} async-done(((bf16[128,3072]{1,0:T(8,128)(2,1)}), bf16[1024,3072]{1,0:T(8,128)(2,1)}) %all-gather.16.cloned.1.call-update) | async-done | bytes 6291472 | tf_op jit(solution)/shard_map/all_gather | solution.py:126
  134.1 17.6 all-gather.2
  151.7 16.7 all-gather.3
  168.5 26.0 %all-gather.5 = bf16[8,1,512]{2,1,0:T(2,128)(2,1)S(1)} all-gather(bf16[1,1,512]{2,1,0:T(2,128)(2,1)S(1)} %reshape.159), channel_id=1, replica_groups=mesh['fsdp'=8,'seq'=4] {'fsdp'}, dimensions={0}, use_global_device_ids=true | all-gather | bytes 9216 | tf_op jit(solution)/shard_map/all_gather | solution.py:163
  194.5 16.2 all-gather.4
  210.7 18.2 all-gather.6
  228.8 16.2 all-gather.7
  245.1 18.5 all-gather.8
  281.7 77.1 %while.28 = (s32[]{:T(128)}, bf16[8,3,256,128]{2,3,0,1:T(8,128)(2,1)}, f32[8,3,2,256,1]{3,2,1,4,0:T(2,128)S(1)}, s32[8]{0:T(128)S(1)}, bf16[3,1024,1024]{1,2,0:T...) while((s32[]{:T(128)}, ...), condition=%wide.region_3.4_spmd.clone, body=%wide.region_0.3_spmd.clone.sunk | while | flops 422312448 | bytes 27983556 | solution.py:147
  365.0 28.9 %all-gather.24.cloned.1.call-done = bf16[1024,4096]{1,0:T(8,128)(2,1)} async-done(((bf16[128,4096]{1,0:T(8,128)(2,1)}), bf16[1024,4096]{1,0:T(8,128)(2,1)}) %all-gather.24.cloned.1.call-update) | async-done | bytes 8388624 | tf_op jit(solution)/shard_map/all_gather | solution.py:162
  393.8 15.5 fusion.45
  413.8 32.0 %multiply_convert_fusion.1 = (bf16[3,256,4096]{2,1,0:T(8,128)(2,1)}, f32[3,256,4096]{2,1,0:T(8,128)}) fusion(f32[3,256,4096]{2,1,0:T(8,128)S(1)} %get-tuple-element.373, f32[4096]{0:T(1024)S(1)} %bitcast.225, u8[256,4096]{1,0:T(8,128)(4,1)} %get-tuple-element.281, u8[256,4096]{1,0:T(8,128)(4,1)} %get-tuple-element.280), kind=kLoop, calls=%fused_computation.44 | loop fusion | flops 223346688 | bytes 33570816 | tf_op jit(solution)/shard_map/convert_element_type | solution.py:172
  445.8 73.2 %all-gather.26.cloned.1.call-done = bf16[4096,1024]{1,0:T(8,128)(2,1)} async-done(((bf16[512,1024]{1,0:T(8,128)(2,1)}), bf16[4096,1024]{1,0:T(8,128)(2,1)}) %all-gather.26.cloned.1.call-update) | async-done | bytes 8388624 | tf_op jit(solution)/shard_map/all_gather | solution.py:164
  536.3 21.3 %convert_reduce_fusion = (f32[4096]{0:T(1024)}, bf16[3,256,4096]{2,1,0:T(8,128)(2,1)}) fusion(f32[3,256,4096]{2,1,0:T(8,128)} %get-tuple-element.359, bf16[3,256,1024]{2,1,0:T(8,128)(2,1)} %get-tuple-element.355, bf16[4096,1024]{1,0:T(8,128)(2,1)} %all-gather.26.cloned.1.call-done, f32[3,256,4096]{2,1,0:T(8,128)} %copy-done.3, f32[4096]{0:T(1024)S(1)} %bitcast.226), kind=kOutput, calls=%fused_computation.42 | convolution fusion | flops 6495924224 | bytes 41451520 | tf_op jit(solution)/shard_map/sbd,fd->sbf/dot_general | solution.py:193
  557.6 14.0 multiply_reduce_fusion.1
  577.6 175.9 %while.29 = (s32[]{:T(128)}, bf16[8,3,256,128]{2,3,1,0:T(8,128)(2,1)S(1)}, bf16[8,3,1024,128]{2,3,1,0:T(8,128)(2,1)}, bf16[8,3,1024,128]{2,3,1,0:T(8,128)(2,1)},...) while((s32[]{:T(128)}, ...), condition=%wide.region_14.15_spmd.clone, body=%wide.region_12.14_spmd.clone.sunk | while | flops 1031993856 | bytes 82044696 | solution.py:219
  837.6 53.6 %reduce-scatter.9.cloned.1.call-done = bf16[3,256,1024]{2,1,0:T(8,128)(2,1)} async-done(((bf16[3,1024,1024]{2,1,0:T(8,128)(2,1)}), bf16[3,256,1024]{2,1,0:T(8,128)(2,1)}) %reduce-scatter.9.cloned.1.call-update) | async-done | bytes 1572880 | tf_op jit(solution)/shard_map/reduce_scatter | solution.py:229
  908.2 74.8 %reduce-scatter.13.cloned.1.call-done = f32[128,1024]{1,0:T(8,128)} async-done(((f32[1024,1024]{1,0:T(8,128)}), f32[128,1024]{1,0:T(8,128)}) %reduce-scatter.13.cloned.1.call-update) | async-done | bytes 524304 | tf_op jit(solution)/shard_map/reduce_scatter | solution.py:251
  986.4 283.2 %reduce-scatter.15.cloned.1.call-done = f32[128,4096]{1,0:T(8,128)} async-done(((f32[1024,4096]{1,0:T(8,128)}), f32[128,4096]{1,0:T(8,128)}) %reduce-scatter.15.cloned.1.call-update) | async-done | bytes 2097168 | tf_op jit(solution)/shard_map/reduce_scatter | solution.py:255
  1272.3 282.8 %reduce-scatter.17.cloned.1.call-done = f32[512,1024]{1,0:T(8,128)} async-done(((f32[4096,1024]{1,0:T(8,128)}), f32[512,1024]{1,0:T(8,128)}) %reduce-scatter.17.cloned.1.call-update) | async-done | bytes 2097168 | tf_op jit(solution)/shard_map/reduce_scatter | solution.py:257
  1557.8 207.9 %reduce-scatter.11.cloned.1.call-done = f32[128,3072]{0,1:T(8,128)} async-done(((f32[1024,3072]{0,1:T(8,128)}), f32[128,3072]{0,1:T(8,128)}) %reduce-scatter.11.cloned.1.call-update) | async-done | bytes 1572880 | tf_op jit(solution)/shard_map/reduce_scatter | solution.py:248
  1768.2 35.6 %all-reduce.9 = (bf16[1024]{0:T(1024)(128)(2,1)S(1)}, bf16[1024]{0:T(1024)(128)(2,1)S(1)}, bf16[1024]{0:T(1024)(128)(2,1)S(1)}, bf16[1024]{0:T(1024)(128)(2,1)S(...) all-reduce(f32[1024]{0:T(1024)S(1)} %bitcast.230, ...), channel_id=5, replica_groups=mesh['fsdp'=8,'seq'=4] {'fsdp'}, use_global_device_ids=true, to_apply=%region_20.21.clone | all-reduce | flops 12288 | bytes 73728
  (426 shorter events, 468.5 us)
Async XLA Ops:
  7.2 104.8 %all-gather.16.cloned.1.call-start = ((), (), s32[]{:S(2)}) async-start(), calls=%async_computation.6 | async-start | bytes 7077888 | tf_op jit(solution)/shard_map/all_gather | solution.py:126
  7.9 256.3 %all-gather.18.cloned.1.call-start = ((), (), s32[]{:S(2)}) async-start(), calls=%async_computation.7 | async-start | bytes 7864320 | tf_op jit(solution)/shard_map/all_gather | solution.py:142
  123.7 149.2 %all-gather.20.cloned.1.call-start = ((), (), s32[]{:S(2)}) async-start(), calls=%async_computation.8 | async-start | bytes 7864320 | tf_op jit(solution)/shard_map/all_gather | solution.py:141
  127.1 231.8 %all-gather.22.cloned.1.call-start = ((), (), s32[]{:S(2)}) async-start(), calls=%async_computation.9 | async-start | bytes 2359296 | tf_op jit(solution)/shard_map/all_gather | solution.py:129
  127.7 266.2 %all-gather.24.cloned.1.call-start = ((), (), s32[]{:S(2)}) async-start(), calls=%async_computation.10 | async-start | bytes 9437184 | tf_op jit(solution)/shard_map/all_gather | solution.py:162
  128.2 390.7 %all-gather.26.cloned.1.call-start = ((), (), s32[]{:S(2)}) async-start(), calls=%async_computation.11 | async-start | bytes 9437184 | tf_op jit(solution)/shard_map/all_gather | solution.py:164
  128.8 706.1 %reduce-scatter.7.cloned.1.call-start = ((), (), s32[]{:S(2)}) async-start(), calls=%async_computation.12 | async-start | bytes 7864320 | tf_op jit(solution)/shard_map/reduce_scatter | solution.py:226
  210.7 308.3 %copy-start.13 = (f32[8,1,128]{2,1,0:T(1,128)}, f32[8,1,128]{2,1,0:T(1,128)S(1)}, u32[]{:S(2)}) copy-start(f32[8,1,128]{2,1,0:T(1,128)S(1)} %convert_element_type.276) | copy-start | bytes 12292
  364.5 207.1 %copy-start = (f32[3,256,1024]{2,1,0:T(8,128)}, f32[3,256,1024]{2,1,0:T(8,128)S(1)}, u32[]{:S(2)}) copy-start(f32[3,256,1024]{2,1,0:T(8,128)S(1)} %get-tuple-element.372) | copy-start | bytes 9437188
  773.4 117.8 %reduce-scatter.9.cloned.1.call-start = ((), (), s32[]{:S(2)}) async-start(), calls=%async_computation.13 | async-start | bytes 7864320 | tf_op jit(solution)/shard_map/reduce_scatter | solution.py:229
  793.2 189.7 %reduce-scatter.13.cloned.1.call-start = ((), (), s32[]{:S(2)}) async-start(), calls=%async_computation.15 | async-start | bytes 4718592 | tf_op jit(solution)/shard_map/reduce_scatter | solution.py:251
  799.3 470.3 %reduce-scatter.15.cloned.1.call-start = ((), (), s32[]{:S(2)}) async-start(), calls=%async_computation.16 | async-start | bytes 18874368 | tf_op jit(solution)/shard_map/reduce_scatter | solution.py:255
  812.9 742.2 %reduce-scatter.17.cloned.1.call-start = ((), (), s32[]{:S(2)}) async-start(), calls=%async_computation.17 | async-start | bytes 18874368 | tf_op jit(solution)/shard_map/reduce_scatter | solution.py:257
  825.6 940.2 %reduce-scatter.11.cloned.1.call-start = ((), (), s32[]{:S(2)}) async-start(), calls=%async_computation.14 | async-start | bytes 14155776 | tf_op jit(solution)/shard_map/reduce_scatter | solution.py:248
  903.9 933.9 %all-reduce.14.cloned.1.call-start = ((), (), s32[]{:S(2)}) async-start(), calls=%async_computation.18 | async-start | bytes 6291456 | tf_op jit(solution)/shard_map/psum | solution.py:263
  1272.2 495.9 %copy-start.16 = (f32[1024]{0:T(1024)S(1)}, f32[1024]{0:T(1024)}, u32[]{:S(2)}) copy-start(f32[1024]{0:T(1024)} %get-tuple-element.354) | copy-start | bytes 12292
  1272.2 495.9 %copy-start.17 = (f32[1024]{0:T(1024)S(1)}, f32[1024]{0:T(1024)}, u32[]{:S(2)}) copy-start(f32[1024]{0:T(1024)} %get-tuple-element.356) | copy-start | bytes 12292
  1272.2 495.9 %copy-start.22 = (f32[4096]{0:T(1024)S(1)}, f32[4096]{0:T(1024)}, u32[]{:S(2)}) copy-start(f32[4096]{0:T(1024)} %get-tuple-element.377) | copy-start | bytes 49156
  1272.2 495.9 %copy-start.23 = (f32[1024]{0:T(1024)S(1)}, f32[1024]{0:T(1024)}, u32[]{:S(2)}) copy-start(f32[1024]{0:T(1024)} %get-tuple-element.284) | copy-start | bytes 12292
  1272.2 495.9 %copy-start.24 = (f32[1024]{0:T(1024)S(1)}, f32[1024]{0:T(1024)}, u32[]{:S(2)}) copy-start(f32[1024]{0:T(1024)} %get-tuple-element.289) | copy-start | bytes 12292
  1272.2 495.9 %copy-start.25 = (f32[1024]{0:T(1024)S(1)}, f32[1024]{0:T(1024)}, u32[]{:S(2)}) copy-start(f32[1024]{0:T(1024)} %get-tuple-element.282) | copy-start | bytes 12292
  1272.2 495.9 %copy-start.26 = (f32[1024]{0:T(1024)S(1)}, f32[1024]{0:T(1024)}, u32[]{:S(2)}) copy-start(f32[1024]{0:T(1024)} %get-tuple-element.287) | copy-start | bytes 12292
  1272.3 542.9 %copy-start.19 = (f32[3,256]{1,0:T(4,128)S(1)}, f32[3,256]{1,0:T(4,128)}, u32[]{:S(2)}) copy-start(f32[3,256]{1,0:T(4,128)} %copy-done.18) | copy-start | bytes 9220
  1272.3 542.9 %copy-start.21 = (f32[3,256]{1,0:T(4,128)S(1)}, f32[3,256]{1,0:T(4,128)}, u32[]{:S(2)}) copy-start(f32[3,256]{1,0:T(4,128)} %copy-done.20) | copy-start | bytes 9220
  (41 other events, 648.5 us)
Sparse Core Ops, SparseCore 0:
  10.2 101.7 all-gather.15
  123.8 44.6 all-gather.17
  170.6 46.3 all-gather.19
  219.0 49.3 all-gather.21
  270.4 123.3 all-gather.23
  395.8 123.1 all-gather.25
  773.5 56.5 reduce-scatter.6
  832.8 58.3 reduce-scatter.8
  894.8 88.0 reduce-scatter.12
  987.0 282.4 reduce-scatter.14
  1273.3 281.7 reduce-scatter.16
  1559.0 206.7 reduce-scatter.10
  1769.7 68.1 all-reduce.13
where the time goes:
time: 1860 us; the launch traced here: 1850 us
  waiting for transfers between devices  1080 us (58%)
  matrix products  260 us (14%)
  blocking collectives  215 us (12%)
  local copies, waits for them, and re-layouts  161 us (9%)
  other arithmetic  105 us (6%)
    reduce_scatter x1, waiting for transfers between devices, body(): lax.psum_scatter(grad_up, 'fsdp', scatter_dimension=0, tiled=True)  283 us
    reduce_scatter x1, waiting for transfers between devices, body(): lax.psum_scatter(grad_down, 'fsdp', scatter_dimension=0, tiled=True)  283 us
    reduce_scatter x1, waiting for transfers between devices, body(): lax.psum_scatter(grad_qkv, 'fsdp', scatter_dimension=0, tiled=True)  208 us
    reduce_scatter x1, waiting for transfers between devices, body(): lax.psum_scatter(grad_out, 'fsdp', scatter_dimension=0, tiled=True)  74.8 us
    all_gather x1, waiting for transfers between devices, body(): lax.all_gather(down_weight, 'fsdp', axis=0, tiled=True)  73.2 us
    all_gather x1, waiting for transfers between devices, body(): lax.all_gather(qkv_weight, 'fsdp', axis=0, tiled=True)  64.9 us
    reduce_scatter x1, waiting for transfers between devices, body(): lax.psum_scatter(join_heads(grad_values_all).astype(jnp.bfloat16), 'seq',...  53.6 us
    dynamic_slice x56, local copies, waits for them, and re-layouts, head_slice(): lax.dynamic_slice_in_dim(array, head_index * group_width, group_width, 2)  47.8 us
  transfers between devices with their start and end apart: 13, of which 9 were waited for; matrix products, arithmetic and copies ran while one was open for 13% of the time, Pallas kernels for 0%

commit v1 on v0

v1 whole, which is shorter than its diff:
```python
import math

import jax
import jax.numpy as jnp
from jax import lax
from jax.experimental import pallas as pl
from jax.experimental.pallas import tpu as pltpu
from jax.sharding import PartitionSpec as P

DH = 64
QBLK = 256
norm_epsilon = 1e-05
masked_score = -1e30
F32 = jnp.float32
BF16 = jnp.bfloat16
NT = (((1,), (1,)), ((), ()))
TN = (((0,), (0,)), ((), ()))
NN = (((1,), (0,)), ((), ()))


def dot(a, b, dims=NN):
    return lax.dot_general(a, b, dims, preferred_element_type=F32)


def attend_kernel(q_ref, k_ref, v_ref, seg_col, seg_row, o_ref, lse_ref):
    heads = q_ref.shape[1] // DH
    allowed = seg_col[...] == seg_row[...]
    for h in range(heads):
        cols = slice(h * DH, (h + 1) * DH)
        scores = dot(k_ref[:, cols], q_ref[:, cols], NT)
        scores = jnp.where(allowed, scores, masked_score)
        peak = jnp.max(scores, axis=0, keepdims=True)
        raw = jnp.exp(scores - peak)
        total = jnp.sum(raw, axis=0, keepdims=True)
        part = dot(v_ref[:, cols], raw.astype(BF16), TN) / total
        o_ref[:, cols] = part.T.astype(BF16)
        lse_ref[h : h + 1, :] = peak + jnp.log(total)


def attend(qkv, seg_col, seg_row):
    length, width = qkv.shape[0], qkv.shape[1] // 3
    heads = width // DH
    return pl.pallas_call(
        attend_kernel,
        grid=(length // QBLK,),
        in_specs=[
            pl.BlockSpec((QBLK, width), lambda i: (i, 0)),
            pl.BlockSpec((length, width), lambda i: (0, 1)),
            pl.BlockSpec((length, width), lambda i: (0, 2)),
            pl.BlockSpec((length, 1), lambda i: (0, 0)),
            pl.BlockSpec((1, QBLK), lambda i: (0, i)),
        ],
        out_specs=[
            pl.BlockSpec((QBLK, width), lambda i: (i, 0)),
            pl.BlockSpec((heads, QBLK), lambda i: (0, i)),
        ],
        out_shape=[
            jax.ShapeDtypeStruct((length, width), BF16),
            jax.ShapeDtypeStruct((heads, length), F32),
        ],
        compiler_params=pltpu.CompilerParams(vmem_limit_bytes=40 * 2**20),
        cost_estimate=pl.CostEstimate(
            flops=16 * heads * length * length * DH,
            bytes_accessed=8 * length * width,
            transcendentals=heads * length * length,
        ),
    )(qkv, qkv, qkv, seg_col, seg_row)


def back_kernel(q_ref, k_ref, v_ref, do_ref, lse_ref, seg_col, seg_row, out_ref, dk_acc, dv_acc):
    step = pl.program_id(0)
    width = q_ref.shape[1]
    heads = width // DH

    @pl.when(step == 0)
    def _():
        dk_acc[...] = jnp.zeros_like(dk_acc)
        dv_acc[...] = jnp.zeros_like(dv_acc)

    allowed = seg_col[...] == seg_row[...]
    rows = pl.ds(pl.multiple_of(step * QBLK, QBLK), QBLK)
    for h in range(heads):
        cols = slice(h * DH, (h + 1) * DH)
        queries, keys, grads = q_ref[:, cols], k_ref[:, cols], do_ref[:, cols]
        scores = dot(keys, queries, NT)
        soft = jnp.exp(jnp.where(allowed, scores, masked_score) - lse_ref[h : h + 1, :])
        grad_soft = dot(v_ref[:, cols], grads, NT)
        inner = jnp.sum(soft * grad_soft, axis=0, keepdims=True)
        grad_scores = (soft * (grad_soft - inner)).astype(BF16)
        dk_acc[:, cols] += dot(grad_scores, queries)
        dv_acc[:, cols] += dot(soft.astype(BF16), grads)
        grad_query = dot(keys, grad_scores, TN) * DH ** (-0.5)
        out_ref[rows, cols] = grad_query.T.astype(BF16)

    @pl.when(step == pl.num_programs(0) - 1)
    def _():
        out_ref[:, width : 2 * width] = dk_acc[...].astype(BF16)
        out_ref[:, 2 * width :] = dv_acc[...].astype(BF16)


def attend_back(qkv, grad_context, lse, seg_col, seg_row):
    length, width = qkv.shape[0], qkv.shape[1] // 3
    heads = width // DH
    return pl.pallas_call(
        back_kernel,
        grid=(length // QBLK,),
        in_specs=[
            pl.BlockSpec((QBLK, width), lambda i: (i, 0)),
            pl.BlockSpec((length, width), lambda i: (0, 1)),
            pl.BlockSpec((length, width), lambda i: (0, 2)),
            pl.BlockSpec((QBLK, width), lambda i: (i, 0)),
            pl.BlockSpec((heads, QBLK), lambda i: (0, i)),
            pl.BlockSpec((length, 1), lambda i: (0, 0)),
            pl.BlockSpec((1, QBLK), lambda i: (0, i)),
        ],
        out_specs=pl.BlockSpec((length, 3 * width), lambda i: (0, 0)),
        out_shape=jax.ShapeDtypeStruct((length, 3 * width), BF16),
        scratch_shapes=[pltpu.VMEM((length, width), F32), pltpu.VMEM((length, width), F32)],
        compiler_params=pltpu.CompilerParams(vmem_limit_bytes=40 * 2**20),
        cost_estimate=pl.CostEstimate(
            flops=40 * heads * length * length * DH,
            bytes_accessed=14 * length * width,
            transcendentals=heads * length * length,
        ),
    )(qkv, qkv, qkv, grad_context, lse, seg_col, seg_row)


def norm_rows(values):
    row_mean = jnp.mean(values, -1, keepdims=True)
    centered = values - row_mean
    inverse = lax.rsqrt(jnp.mean(centered * centered, -1, keepdims=True) + norm_epsilon)
    return centered * inverse, inverse


def norm_back(upstream, normed, inverse, gain):
    scaled = upstream * gain
    first_mean = jnp.mean(scaled, -1, keepdims=True)
    second_mean = jnp.mean(scaled * normed, -1, keepdims=True)
    return inverse * (scaled - first_mean - normed * second_mean)


def make_body(n, k):
    def swap(array, flip):
        return lax.ppermute(array, "seq", [(i, i ^ flip) for i in range(k)])

    def gather(own):
        near = swap(own, 1)
        far = swap(own, 2)
        return jnp.concatenate([own, near, far, swap(far, 1)], axis=0)

    def scatter(partial):
        rows = partial.shape[0] // k
        low = partial.astype(BF16)
        block = lambda j: low[j * rows : (j + 1) * rows]
        got = swap(jnp.concatenate([block(1), block(3)], axis=0), 1)
        exact = lambda j: partial[j * rows : (j + 1) * rows]
        other = swap((exact(2) + got[rows:].astype(F32)).astype(BF16), 2)
        return exact(0) + got[:rows].astype(F32) + other.astype(F32)

    def exchange(blocks):
        me = lax.axis_index("seq")
        return [blocks(me)] + [swap(blocks(me ^ d), d) for d in range(1, k)]

    def absolute(pieces):
        me = lax.axis_index("seq")
        stacked = jnp.stack(pieces)
        return [lax.dynamic_index_in_dim(stacked, me ^ t, 0, keepdims=False) for t in range(k)]

    def body(
        tokens,
        segments,
        qkv_weight,
        query_bias,
        value_bias,
        out_weight,
        out_bias,
        first_gain,
        first_shift,
        hidden_weight,
        hidden_bias,
        down_weight,
        down_bias,
        second_gain,
        second_shift,
        cotangent,
    ):
        me = lax.axis_index("seq")
        seqs, blk, D = tokens.shape
        FF = hidden_weight.shape[1]
        wide = D // k
        units = FF // k
        shard = D // n
        unit_shard = units // n

        small = jnp.concatenate(
            [
                query_bias,
                value_bias,
                out_bias,
                first_gain,
                first_shift,
                down_bias,
                second_gain,
                second_shift,
                hidden_bias,
            ]
        )
        count = small.shape[0]
        extra = 16
        small = jnp.pad(small, (0, extra * 3 * wide - count)).reshape(extra, 3 * wide)
        mine = lax.dynamic_index_in_dim(
            qkv_weight.reshape(shard, 3, k, wide), me, 2, keepdims=False
        ).reshape(shard, 3 * wide)
        packed = lax.all_gather(jnp.concatenate([mine, small], axis=0), "fsdp", axis=0)
        w_qkv = packed[:, :shard].reshape(D, 3 * wide)
        vectors = packed[:, shard:].reshape(n, extra * 3 * wide)[:, :count].astype(F32)
        vector = lambda j: vectors[:, j * shard : (j + 1) * shard].reshape(1, D)
        (qbias, vbias, obias, gain_one, shift_one, dbias, gain_two, shift_two) = [
            vector(j) for j in range(8)
        ]
        hbias = lax.dynamic_index_in_dim(
            vectors[:, 8 * shard :].reshape(n, k, unit_shard), me, 1, keepdims=False
        ).reshape(1, units)
        own_columns = lambda v: lax.dynamic_slice_in_dim(v, me * wide, wide, 1)
        qkv_bias = jnp.concatenate(
            [own_columns(qbias), jnp.zeros((1, wide), F32), own_columns(vbias)], axis=1
        )
        qkv_scale = jnp.concatenate(
            [jnp.full((1, wide), DH ** (-0.5), F32), jnp.ones((1, 2 * wide), F32)], axis=1
        )

        out_mine = lax.dynamic_slice_in_dim(out_weight, me * wide, wide, 1)
        out_columns = lax.all_gather(out_mine, "fsdp", axis=0, tiled=True)
        w_out = jnp.concatenate(
            absolute(exchange(lambda t: lax.dynamic_slice_in_dim(out_columns, t * wide, wide, 0))),
            axis=1,
        )
        up_mine = lax.dynamic_index_in_dim(
            hidden_weight.reshape(shard, n, k, unit_shard), me, 2, keepdims=False
        ).reshape(shard, units)
        w_up = lax.all_gather(up_mine, "fsdp", axis=0, tiled=True)
        down_mine = lax.dynamic_slice_in_dim(down_weight, me * unit_shard, unit_shard, 0)
        w_down = lax.all_gather(down_mine, "fsdp", axis=0, tiled=True)

        seg_all = jnp.concatenate(
            [segments, swap(segments, 1), swap(segments, 2), swap(segments, 3)], axis=1
        )

        state = []
        for i in range(seqs):
            x = gather(tokens[i])
            seg_col, seg_row = seg_all[i][:, None], seg_all[i][None, :]
            qkv = ((dot(x, w_qkv) + qkv_bias) * qkv_scale).astype(BF16)
            context, lse = attend(qkv, seg_col, seg_row)
            state.append([x, seg_col, seg_row, qkv, context, lse, scatter(dot(context, w_out))])
        for i in range(seqs):
            attention = state[i][-1] + obias
            normed_one, inverse_one = norm_rows(tokens[i].astype(F32) + attention)
            hidden = normed_one * gain_one + shift_one
            hid = gather(hidden.astype(BF16))
            pre = dot(hid, w_up) + hbias
            cdf = 0.5 * (1.0 + lax.erf(pre * math.sqrt(0.5)))
            act = (pre * cdf).astype(BF16)
            slope = (cdf + pre * (jnp.exp(-0.5 * pre * pre) / math.sqrt(2 * math.pi))).astype(BF16)
            branch = scatter(dot(act, w_down))
            state[i] += [normed_one, inverse_one, hidden, hid, act, slope, branch]

        outs, grad_tokens = [], []
        sums = [0.0] * 6
        g_down = g_up = g_out = g_qkv = 0.0
        s_pre = s_qkv = 0.0
        grads = []
        total = lambda a: jnp.sum(a, axis=0)
        for i in range(seqs):
            normed_one, inverse_one, hidden, hid, act, slope, branch = state[i][7:]
            normed_two, inverse_two = norm_rows(hidden + branch + dbias)
            outs.append((normed_two * gain_two + shift_two).astype(BF16))
            upstream = cotangent[i].astype(F32)
            grad_two = norm_back(upstream, normed_two, inverse_two, gain_two)
            grad_branch = grad_two.astype(BF16)
            sums[3] += total(grad_branch.astype(F32))
            sums[4] += total(upstream * normed_two)
            sums[5] += total(upstream)
            gb = gather(grad_branch)
            g_down += dot(act, gb, TN)
            grad_pre = (dot(gb, w_down, NT) * slope.astype(F32)).astype(BF16)
            s_pre += total(grad_pre.astype(F32))
            g_up += dot(hid, grad_pre, TN)
            grad_hidden = grad_two + scatter(dot(grad_pre, w_up, NT))
            grads.append(grad_hidden)

        def shared(grad):
            return lax.psum_scatter(grad.astype(BF16), "fsdp", scatter_dimension=0, tiled=True)

        r_down = shared(g_down)
        r_up = shared(g_up)

        for i in range(seqs):
            x, seg_col, seg_row, qkv, context, lse = state[i][:6]
            normed_one, inverse_one = state[i][7:9]
            grad_hidden = grads[i]
            grad_one = norm_back(grad_hidden, normed_one, inverse_one, gain_one)
            grad_attention = grad_one.astype(BF16)
            sums[0] += total(grad_attention.astype(F32))
            sums[1] += total(grad_hidden * normed_one)
            sums[2] += total(grad_hidden)
            ga = gather(grad_attention)
            g_out += dot(context, ga, TN)
            grad_context = dot(ga, w_out, NT).astype(BF16)
            dqkv = attend_back(qkv, grad_context, lse, seg_col, seg_row)
            s_qkv += total(dqkv.astype(F32))
            g_qkv += dot(x, dqkv, TN)
            grad_tokens.append(grad_one + scatter(dot(dqkv, w_qkv, NT)))

        g_out = g_out.astype(BF16)
        r_out = shared(
            jnp.concatenate(
                absolute(exchange(lambda t: lax.dynamic_slice_in_dim(g_out, t * wide, wide, 1))),
                axis=0,
            )
        )

        place = lambda v: lax.dynamic_update_slice_in_dim(
            jnp.zeros((D,), F32), v, me * wide, 0
        )
        full = [place(s_qkv[:wide]), place(s_qkv[2 * wide :])] + sums
        hidden_sum = lax.dynamic_update_slice_in_dim(
            jnp.zeros((n, k, unit_shard), F32), s_pre.reshape(n, 1, unit_shard), me, 1
        ).reshape(n, k * unit_shard)
        vector_sums = jnp.concatenate([v.reshape(n, shard) for v in full] + [hidden_sum], axis=1)
        vector_sums = jnp.pad(vector_sums, ((0, 0), (0, extra * 3 * wide - count)))
        joined = jnp.concatenate(
            [
                g_qkv.astype(BF16).reshape(n, shard, 3 * wide),
                vector_sums.astype(BF16).reshape(n, extra, 3 * wide),
            ],
            axis=1,
        )
        r_qkv = lax.psum_scatter(joined, "fsdp", scatter_dimension=0, tiled=True)[0]

        every = lambda a: lax.all_gather(a, "seq", axis=0)
        all_down = every(r_down).reshape(k * unit_shard, D).astype(F32)
        all_up = (
            every(r_up)
            .reshape(k, shard, n, unit_shard)
            .transpose(1, 2, 0, 3)
            .reshape(shard, FF)
            .astype(F32)
        )
        all_out = every(r_out).transpose(1, 0, 2).reshape(shard, D).astype(F32)
        last = every(r_qkv)
        all_qkv = (
            last[:, :shard]
            .reshape(k, shard, 3, wide)
            .transpose(1, 2, 0, 3)
            .reshape(shard, 3 * D)
            .astype(F32)
        )
        vec = jnp.sum(last[:, shard:].astype(F32), axis=0).reshape(-1)[:count]
        piece = lambda j: vec[j * shard : (j + 1) * shard]
        return (
            jnp.stack(outs),
            jnp.stack(grad_tokens),
            all_qkv,
            piece(0),
            piece(1),
            all_out,
            piece(2),
            piece(3),
            piece(4),
            all_up,
            vec[8 * shard :],
            all_down,
            piece(5),
            piece(6),
            piece(7),
        )

    return body


def solution(mesh):
    rows = P("fsdp", "seq", None)
    matrix, vector = P("fsdp", None), P("fsdp")
    weights = (
        matrix,
        vector,
        vector,
        matrix,
        vector,
        vector,
        vector,
        matrix,
        vector,
        matrix,
        vector,
        vector,
        vector,
    )
    return jax.shard_map(
        make_body(mesh.shape["fsdp"], mesh.shape["seq"]),
        mesh=mesh,
        in_specs=(rows, P("fsdp", "seq")) + weights + (rows,),
        out_specs=(rows, rows) + weights,
        check_vma=False,
    )
```

time: 1860 us -> 745 us (0.40)
  waiting for transfers between devices: 1080 us -> 295 us
  blocking collectives: 215 us -> 60.1 us
  matrix products: 260 us -> 124 us
  local copies, waits for them, and re-layouts: 161 us -> 47 us
  Pallas kernels: 0 us -> 91.2 us
  other arithmetic: 105 us -> 57.3 us
  starting transfers between devices: 0.52 us -> 47.6 us
    reduce_scatter x6 -> x4, waiting for transfers between devices: 902 us -> 84.2 us  [the longest x1 67.6 us: body(): r_qkv = lax.psum_scatter(joined, 'fsdp', scatter_dimension=0, tiled=True)[0]]
    ppermute x0 -> x69, waiting for transfers between devices: none -> 205 us  [swap(): return lax.ppermute(array, 'seq', [(i, i ^ flip) for i in range(k)])]
    all_gather x6 -> x5, waiting for transfers between devices: 167 us -> 5.53 us  [the longest x2 5.5 us: body(): every = lambda a: lax.all_gather(a, 'seq', axis=0)]
    dot_general x68 -> x36, matrix products: 260 us -> 124 us  [dot(): return lax.dot_general(a, b, dims, preferred_element_type=F32)]
    all_gather x10 -> x3, blocking collectives: 174 us -> 60.1 us  [the longest x1 32.9 us: body(): out_columns = lax.all_gather(out_mine, 'fsdp', axis=0, tiled=True)]
    pallas_call x0 -> x6, Pallas kernels: none -> 91.2 us  [the longest x3 52.6 us: attend_back(): pl.pallas_call(back_kernel, grid=(length // QBLK,), in_specs=[pl.BlockSpe...]
    convert_element_type x35 -> x17, other arithmetic: 71.2 us -> 15.5 us  [the longest x12 11.3 us: scatter(): other = swap((exact(2) + got[rows:].astype(F32)).astype(BF16), 2)]
    dynamic_slice x72 -> x5, local copies, waits for them, and re-layouts: 57.2 us -> 3.23 us  [the longest x1 0.94 us: body(): lax.dynamic_index_in_dim(qkv_weight.reshape(shard, 3, k, wide), me, 2, ke...]
  transfers between devices with their start and end apart: 13 -> 78, of which waited for: 9 -> 27; matrix products, arithmetic and copies ran while one was open for 13% -> 24% of each run, Pallas kernels for 0% -> 12%
where the time goes in v1:
time: 745 us; the launch traced here: 739 us
  waiting for transfers between devices  295 us (40%)
  matrix products  124 us (17%)
  Pallas kernels  91.2 us (12%)
  blocking collectives  60.1 us (8%)
  other arithmetic  57.3 us (8%)
  starting transfers between devices  47.6 us (6%)
  local copies, waits for them, and re-layouts  47 us (6%)
  between operations  16.5 us (2%)
    ppermute x69, waiting for transfers between devices, swap(): return lax.ppermute(array, 'seq', [(i, i ^ flip) for i in range(k)])  205 us
    dot_general x36, matrix products, dot(): return lax.dot_general(a, b, dims, preferred_element_type=F32)  124 us
    reduce_scatter x1, waiting for transfers between devices, body(): r_qkv = lax.psum_scatter(joined, 'fsdp', scatter_dimension=0, tiled=True)[0]  67.6 us
    pallas_call x3, Pallas kernels, attend_back(): pl.pallas_call(back_kernel, grid=(length // QBLK,), in_specs=[pl.BlockSpe...  52.6 us
    ppermute x69, starting transfers between devices, swap(): return lax.ppermute(array, 'seq', [(i, i ^ flip) for i in range(k)])  46.7 us
    pallas_call x3, Pallas kernels, attend(): pl.pallas_call(attend_kernel, grid=(length // QBLK,), in_specs=[pl.BlockS...  38.6 us
    all_gather x1, blocking collectives, body(): out_columns = lax.all_gather(out_mine, 'fsdp', axis=0, tiled=True)  32.9 us
    all_gather x2, blocking collectives, body(): every = lambda a: lax.all_gather(a, 'seq', axis=0)  27.2 us
  transfers between devices with their start and end apart: 78, of which 27 were waited for; matrix products, arithmetic and copies ran while one was open for 24% of the time, Pallas kernels for 12%

profile of v1, /device:TPU:0, one launch (start us, length us, event | category | flops | bytes accessed | tf_op | source)
XLA Modules:
  0.0 739.1 jit_solution(16439373661084890779)
XLA Ops:
  28.9 32.9 %all_gather.38 = bf16[1024,256]{1,0:T(8,128)(2,1)S(1)} all-gather(bf16[128,256]{1,0:T(8,128)(2,1)S(1)} %constant_dynamic-slice_fusion.9), channel_id=1, replica_groups=mesh['fsdp'=8,'seq'=4] {'fsdp'}, dimensions={0}, use_global_device_ids=true | all-gather | bytes 589824 | tf_op jit(solution)/shard_map/all_gather | solution.py:233
  82.9 9.3 %collective-permute-done.17 = bf16[256,1024]{1,0:T(8,128)(2,1)} collective-permute-done((bf16[256,1024]{1,0:T(8,128)(2,1)}, bf16[256,1024]{1,0:T(8,128)(2,1)}, u32[]{:S(2)}, u32[]{:S(2)}) %collective-permute-start.17) | collective-permute-done | bytes 524320 | tf_op jit(solution)/shard_map/ppermute | solution.py:144
  95.6 13.1 %shard_map.271 = (bf16[1024,256]{1,0:T(8,128)(2,1)S(1)}, f32[4,1024]{1,0:T(4,128)S(1)}) custom-call(bf16[1024,768]{1,0:T(8,128)(2,1)S(1)} %multiply_convert_fusion.8.q_ref.k_ref.v_ref, bf16[1024,768]{1,0:T(8,128)(2,1)S(1)} %multiply_convert_fusion.8.q_ref.k_ref.v_ref, bf16[1024,768]{1,0:T(8,128)(2,1)S(1)} %multiply_convert_fusion.8.q_ref.k_ref.v_ref, ...), custom_call_target="tpu_custom_call" | custom-call | flops 4294967296 | bytes 2097152 | tf_op jit(solution)/shard_map/pallas_call | solution.py:43
  114.4 12.7 %shard_map.273 = (bf16[1024,256]{1,0:T(8,128)(2,1)S(1)}, f32[4,1024]{1,0:T(4,128)S(1)}) custom-call(bf16[1024,768]{1,0:T(8,128)(2,1)S(1)} %multiply_convert_fusion.6.q_ref.k_ref.v_ref, bf16[1024,768]{1,0:T(8,128)(2,1)S(1)} %multiply_convert_fusion.6.q_ref.k_ref.v_ref, bf16[1024,768]{1,0:T(8,128)(2,1)S(1)} %multiply_convert_fusion.6.q_ref.k_ref.v_ref, ...), custom_call_target="tpu_custom_call" | custom-call | flops 4294967296 | bytes 2097152 | tf_op jit(solution)/shard_map/pallas_call | solution.py:43
  132.3 12.8 %shard_map.272 = (bf16[1024,256]{1,0:T(8,128)(2,1)S(1)}, f32[4,1024]{1,0:T(4,128)S(1)}) custom-call(bf16[1024,768]{1,0:T(8,128)(2,1)S(1)} %multiply_convert_fusion.7.q_ref.k_ref.v_ref, bf16[1024,768]{1,0:T(8,128)(2,1)S(1)} %multiply_convert_fusion.7.q_ref.k_ref.v_ref, bf16[1024,768]{1,0:T(8,128)(2,1)S(1)} %multiply_convert_fusion.7.q_ref.k_ref.v_ref, ...), custom_call_target="tpu_custom_call" | custom-call | flops 4294967296 | bytes 2097152 | tf_op jit(solution)/shard_map/pallas_call | solution.py:43
  162.8 11.2 %collective-permute-done.30 = bf16[256,1024]{1,0:T(8,128)(2,1)S(1)} collective-permute-done((bf16[256,1024]{1,0:T(8,128)(2,1)}, bf16[256,1024]{1,0:T(8,128)(2,1)S(1)}, u32[]{:S(2)}, u32[]{:S(2)}) %collective-permute-start.30) | collective-permute-done | bytes 524320 | tf_op jit(solution)/shard_map/ppermute | solution.py:144
  174.0 10.6 %collective-permute-done.20 = bf16[256,1024]{1,0:T(8,128)(2,1)S(1)} collective-permute-done((bf16[256,1024]{1,0:T(8,128)(2,1)}, bf16[256,1024]{1,0:T(8,128)(2,1)S(1)}, u32[]{:S(2)}, u32[]{:S(2)}) %collective-permute-start.20) | collective-permute-done | bytes 524320 | tf_op jit(solution)/shard_map/ppermute | solution.py:144
  194.1 13.1 %collective-permute-done.22 = bf16[256,1024]{1,0:T(8,128)(2,1)} collective-permute-done((bf16[256,1024]{1,0:T(8,128)(2,1)}, bf16[256,1024]{1,0:T(8,128)(2,1)}, u32[]{:S(2)}, u32[]{:S(2)}) %collective-permute-start.22) | collective-permute-done | bytes 524320 | tf_op jit(solution)/shard_map/ppermute | solution.py:144
  245.8 10.6 %collective-permute-done.15 = bf16[256,1024]{1,0:T(8,128)(2,1)S(1)} collective-permute-done((bf16[256,1024]{1,0:T(8,128)(2,1)S(1)}, bf16[256,1024]{1,0:T(8,128)(2,1)S(1)}, u32[]{:S(2)}, u32[]{:S(2)}) %collective-permute-start.15) | collective-permute-done | bytes 524320 | tf_op jit(solution)/shard_map/ppermute | solution.py:144
  256.4 10.3 %collective-permute-done.25 = bf16[256,1024]{1,0:T(8,128)(2,1)S(1)} collective-permute-done((bf16[256,1024]{1,0:T(8,128)(2,1)S(1)}, bf16[256,1024]{1,0:T(8,128)(2,1)S(1)}, u32[]{:S(2)}, u32[]{:S(2)}) %collective-permute-start.25) | collective-permute-done | bytes 524320 | tf_op jit(solution)/shard_map/ppermute | solution.py:144
  269.5 11.4 %collective-permute-done.32 = bf16[256,1024]{1,0:T(8,128)(2,1)S(1)} collective-permute-done((bf16[256,1024]{1,0:T(8,128)(2,1)S(1)}, bf16[256,1024]{1,0:T(8,128)(2,1)S(1)}, u32[]{:S(2)}, u32[]{:S(2)}) %collective-permute-start.32) | collective-permute-done | bytes 524320 | tf_op jit(solution)/shard_map/ppermute | solution.py:144
  292.9 12.1 %collective-permute-done.35 = bf16[256,1024]{1,0:T(8,128)(2,1)S(1)} collective-permute-done((bf16[256,1024]{1,0:T(8,128)(2,1)S(1)}, bf16[256,1024]{1,0:T(8,128)(2,1)S(1)}, u32[]{:S(2)}, u32[]{:S(2)}) %collective-permute-start.35) | collective-permute-done | bytes 524320 | tf_op jit(solution)/shard_map/ppermute | solution.py:144
  313.5 11.2 %collective-permute-done.47 = bf16[256,1024]{1,0:T(8,128)(2,1)S(1)} collective-permute-done((bf16[256,1024]{1,0:T(8,128)(2,1)S(1)}, bf16[256,1024]{1,0:T(8,128)(2,1)S(1)}, u32[]{:S(2)}, u32[]{:S(2)}) %collective-permute-start.47) | collective-permute-done | bytes 524320 | tf_op jit(solution)/shard_map/ppermute | solution.py:144
  326.1 9.8 %collective-permute-done.37 = bf16[256,1024]{1,0:T(8,128)(2,1)S(1)} collective-permute-done((bf16[256,1024]{1,0:T(8,128)(2,1)S(1)}, bf16[256,1024]{1,0:T(8,128)(2,1)S(1)}, u32[]{:S(2)}, u32[]{:S(2)}) %collective-permute-start.37) | collective-permute-done | bytes 524320 | tf_op jit(solution)/shard_map/ppermute | solution.py:144
  336.0 9.5 %collective-permute-done.57 = bf16[256,1024]{1,0:T(8,128)(2,1)S(1)} collective-permute-done((bf16[256,1024]{1,0:T(8,128)(2,1)S(1)}, bf16[256,1024]{1,0:T(8,128)(2,1)S(1)}, u32[]{:S(2)}, u32[]{:S(2)}) %collective-permute-start.57) | collective-permute-done | bytes 524320 | tf_op jit(solution)/shard_map/ppermute | solution.py:144
  400.7 10.7 %collective-permute-done.60 = bf16[256,1024]{1,0:T(8,128)(2,1)S(1)} collective-permute-done((bf16[256,1024]{1,0:T(8,128)(2,1)S(1)}, bf16[256,1024]{1,0:T(8,128)(2,1)S(1)}, u32[]{:S(2)}, u32[]{:S(2)}) %collective-permute-start.60) | collective-permute-done | bytes 524320 | tf_op jit(solution)/shard_map/ppermute | solution.py:144
  457.9 16.0 %collective-permute-done.52 = bf16[256,1024]{1,0:T(8,128)(2,1)} collective-permute-done((bf16[256,1024]{1,0:T(8,128)(2,1)S(1)}, bf16[256,1024]{1,0:T(8,128)(2,1)}, u32[]{:S(2)}, u32[]{:S(2)}) %collective-permute-start.52) | collective-permute-done | bytes 524320 | tf_op jit(solution)/shard_map/ppermute | solution.py:144
  485.2 17.2 %shard_map.274 = bf16[1024,768]{1,0:T(8,128)(2,1)S(1)} custom-call(bf16[1024,768]{1,0:T(8,128)(2,1)S(1)} %copy-done.17, bf16[1024,768]{1,0:T(8,128)(2,1)S(1)} %copy-done.17, bf16[1024,768]{1,0:T(8,128)(2,1)S(1)} %copy-done.17, bf16[1024,256]{1,0:T(8,128)(2,1)S(1)} %convolution_convert_fusion.2.do_ref, f32[4,1024]{1,0:T(4,128)S(1)} %get-tuple-element.24.lse_ref, ...), custom_call_target="tpu_custom_call" | custom-call | flops 10737418240 | bytes 3670016 | tf_op jit(solution)/shard_map/pallas_call | solution.py:104
  504.9 16.9 %shard_map.276 = bf16[1024,768]{1,0:T(8,128)(2,1)S(1)} custom-call(bf16[1024,768]{1,0:T(8,128)(2,1)S(1)} %copy-done.19, bf16[1024,768]{1,0:T(8,128)(2,1)S(1)} %copy-done.19, bf16[1024,768]{1,0:T(8,128)(2,1)S(1)} %copy-done.19, bf16[1024,256]{1,0:T(8,128)(2,1)S(1)} %convolution_convert_fusion.do_ref, f32[4,1024]{1,0:T(4,128)S(1)} %get-tuple-element.26.lse_ref, ...), custom_call_target="tpu_custom_call" | custom-call | flops 10737418240 | bytes 3670016 | tf_op jit(solution)/shard_map/pallas_call | solution.py:104
  524.9 18.5 %shard_map.275 = bf16[1024,768]{1,0:T(8,128)(2,1)} custom-call(bf16[1024,768]{1,0:T(8,128)(2,1)S(1)} %copy-done.21, bf16[1024,768]{1,0:T(8,128)(2,1)S(1)} %copy-done.21, bf16[1024,768]{1,0:T(8,128)(2,1)S(1)} %copy-done.21, bf16[1024,256]{1,0:T(8,128)(2,1)S(1)} %convolution_convert_fusion.1.do_ref, f32[4,1024]{1,0:T(4,128)S(1)} %get-tuple-element.25.lse_ref, ...), custom_call_target="tpu_custom_call" | custom-call | flops 10737418240 | bytes 3670016 | tf_op jit(solution)/shard_map/pallas_call | solution.py:104
  592.9 16.6 %reduce-scatter.7.cloned.1.call-done = bf16[128,256]{1,0:T(8,128)(2,1)} async-done(((bf16[1024,256]{1,0:T(8,128)(2,1)}), bf16[128,256]{1,0:T(8,128)(2,1)}) %reduce-scatter.7.cloned.1.call-update) | async-done | bytes 65552 | tf_op jit(solution)/shard_map/reduce_scatter | solution.py:293
  609.5 17.9 %all-gather.1 = bf16[512,256]{1,0:T(8,128)(2,1)S(1)} all-gather(bf16[128,256]{1,0:T(8,128)(2,1)} %reduce-scatter.7.cloned.1.call-done), channel_id=3, replica_groups=mesh['fsdp'=8,'seq'=4] {'seq'}, dimensions={0}, use_global_device_ids=true | all-gather | bytes 327680 | tf_op jit(solution)/shard_map/all_gather | solution.py:341
  652.0 67.6 %reduce-scatter.5.cloned.1.call-done = bf16[1,144,768]{2,1,0:T(8,128)(2,1)} async-done(((bf16[8,144,768]{2,1,0:T(8,128)(2,1)}), bf16[1,144,768]{2,1,0:T(8,128)(2,1)}) %reduce-scatter.5.cloned.1.call-update) | async-done | bytes 221200 | tf_op jit(solution)/shard_map/reduce_scatter | solution.py:339
  719.6 9.3 %all_gather.41 = bf16[4,144,768]{2,1,0:T(8,128)(2,1)S(1)} all-gather(bf16[1,144,768]{2,1,0:T(8,128)(2,1)} %reduce-scatter.5.cloned.1.call-done), channel_id=1, replica_groups=mesh['fsdp'=8,'seq'=4] {'seq'}, dimensions={0}, use_global_device_ids=true | all-gather | bytes 1105920 | tf_op jit(solution)/shard_map/all_gather | solution.py:341
  (589 shorter events, 341.3 us)
Async XLA Ops:
  7.2 65.1 %all-gather.14.cloned.1.call-start = ((), (), s32[]{:S(2)}) async-start(), calls=%async_computation.10 | async-start | bytes 1990656 | tf_op jit(solution)/shard_map/all_gather | solution.py:214
  19.2 197.9 %all-gather.10.cloned.1.call-start = ((), (), s32[]{:S(2)}) async-start(), calls=%async_computation.4 | async-start | bytes 2359296 | tf_op jit(solution)/shard_map/all_gather | solution.py:241
  19.3 42.7 %collective-permute-start.4 = (s32[3,256]{1,0:T(4,128)S(1)}, s32[3,256]{1,0:T(4,128)S(1)}, u32[]{:S(2)}, u32[]{:S(2)}) collective-permute-start(s32[3,256]{1,0:T(4,128)S(1)} %copy-done.75), channel_id=1, source_target_pairs={{0,2},{1,3},{2,0},{3,1},{4,6},{5,7},{6,4},{7,5},{8,10},{9,11},{10,... | collective-permute-start | bytes 9224 | tf_op jit(solution)/shard_map/ppermute | solution.py:144
  22.3 39.6 %collective-permute-start.3 = (s32[3,256]{1,0:T(4,128)S(1)}, s32[3,256]{1,0:T(4,128)S(1)}, u32[]{:S(2)}, u32[]{:S(2)}) collective-permute-start(s32[3,256]{1,0:T(4,128)S(1)} %copy-done.75), channel_id=1, source_target_pairs={{0,1},{1,0},{2,3},{3,2},{4,5},{5,4},{6,7},{7,6},{8,9},{9,8},{10,11... | collective-permute-start | bytes 9224 | tf_op jit(solution)/shard_map/ppermute | solution.py:144
  22.3 40.1 %collective-permute-start.5 = (s32[3,256]{1,0:T(4,128)S(1)}, s32[3,256]{1,0:T(4,128)S(1)}, u32[]{:S(2)}, u32[]{:S(2)}) collective-permute-start(s32[3,256]{1,0:T(4,128)S(1)} %copy-done.75), channel_id=1, source_target_pairs={{0,3},{1,2},{2,1},{3,0},{4,7},{5,6},{6,5},{7,4},{8,11},{9,10},{10,... | collective-permute-start | bytes 9224 | tf_op jit(solution)/shard_map/ppermute | solution.py:144
  23.7 48.3 %collective-permute-start.1 = (bf16[256,1024]{1,0:T(8,128)(2,1)}, bf16[256,1024]{1,0:T(8,128)(2,1)}, u32[]{:S(2)}, u32[]{:S(2)}) collective-permute-start(bf16[256,1024]{1,0:T(8,128)(2,1)} %get-tuple-element.162), channel_id=1, source_target_pairs={{0,2},{1,3},{2,0},{3,1},{4,6},{5,7},{6,4},{7,5},{8,10},{9,11},{10,... | collective-permute-start | bytes 1572872 | tf_op jit(solution)/shard_map/ppermute | solution.py:144
  25.6 49.9 %collective-permute-start = (bf16[256,1024]{1,0:T(8,128)(2,1)}, bf16[256,1024]{1,0:T(8,128)(2,1)}, u32[]{:S(2)}, u32[]{:S(2)}) collective-permute-start(bf16[256,1024]{1,0:T(8,128)(2,1)} %get-tuple-element.162), channel_id=1, source_target_pairs={{0,1},{1,0},{2,3},{3,2},{4,5},{5,4},{6,7},{7,6},{8,9},{9,8},{10,11... | collective-permute-start | bytes 1572872 | tf_op jit(solution)/shard_map/ppermute | solution.py:144
  28.0 203.5 %all-gather.12.cloned.1.call-start = ((), (), s32[]{:S(2)}) async-start(), calls=%async_computation.5 | async-start | bytes 2359296 | tf_op jit(solution)/shard_map/all_gather | solution.py:243
  68.4 41.8 %collective-permute-start.26 = (bf16[256,1024]{1,0:T(8,128)(2,1)}, bf16[256,1024]{1,0:T(8,128)(2,1)}, u32[]{:S(2)}, u32[]{:S(2)}) collective-permute-start(bf16[256,1024]{1,0:T(8,128)(2,1)} %get-tuple-element.163), channel_id=1, source_target_pairs={{0,1},{1,0},{2,3},{3,2},{4,5},{5,4},{6,7},{7,6},{8,9},{9,8},{10,11... | collective-permute-start | bytes 1572872 | tf_op jit(solution)/shard_map/ppermute | solution.py:144
  75.5 52.9 %collective-permute-start.16 = (bf16[256,1024]{1,0:T(8,128)(2,1)}, bf16[256,1024]{1,0:T(8,128)(2,1)S(1)}, u32[]{:S(2)}, u32[]{:S(2)}) collective-permute-start(bf16[256,1024]{1,0:T(8,128)(2,1)} %get-tuple-element.164), channel_id=1, source_target_pairs={{0,1},{1,0},{2,3},{3,2},{4,5},{5,4},{6,7},{7,6},{8,9},{9,8},{10,11... | collective-permute-start | bytes 1572872 | tf_op jit(solution)/shard_map/ppermute | solution.py:144
  92.2 36.2 %collective-permute-start.18 = (bf16[256,1024]{1,0:T(8,128)(2,1)}, bf16[256,1024]{1,0:T(8,128)(2,1)S(1)}, u32[]{:S(2)}, u32[]{:S(2)}) collective-permute-start(bf16[256,1024]{1,0:T(8,128)(2,1)} %collective-permute-done.17), channel_id=1, source_target_pairs={{0,1},{1,0},{2,3},{3,2},{4,5},{5,4},{6,7},{7,6},{8,9},{9,8},{10,11... | collective-permute-start | bytes 1572872 | tf_op jit(solution)/shard_map/ppermute | solution.py:144
  109.7 36.7 %collective-permute-start.9 = (bf16[512,1024]{1,0:T(8,128)(2,1)S(1)}, bf16[512,1024]{1,0:T(8,128)(2,1)S(1)}, u32[]{:S(2)}, u32[]{:S(2)}) collective-permute-start(bf16[512,1024]{1,0:T(8,128)(2,1)S(1)} %pad_maximum_fusion.15), channel_id=1, source_target_pairs={{0,1},{1,0},{2,3},{3,2},{4,5},{5,4},{6,7},{7,6},{8,9},{9,8},{10,11... | collective-permute-start | bytes 3145736 | tf_op jit(solution)/shard_map/ppermute | solution.py:144
  154.6 398.3 %reduce-scatter.9.cloned.1.call-start = ((), (), s32[]{:S(2)}) async-start(), calls=%async_computation.8 | async-start | bytes 2359296 | tf_op jit(solution)/shard_map/reduce_scatter | solution.py:293
  378.1 188.7 %reduce-scatter.11.cloned.1.call-start = ((), (), s32[]{:S(2)}) async-start(), calls=%async_computation.9 | async-start | bytes 2359296 | tf_op jit(solution)/shard_map/reduce_scatter | solution.py:293
  457.3 152.2 %reduce-scatter.7.cloned.1.call-start = ((), (), s32[]{:S(2)}) async-start(), calls=%async_computation.7 | async-start | bytes 589824 | tf_op jit(solution)/shard_map/reduce_scatter | solution.py:293
  481.0 64.5 %collective-permute-start.68 = (bf16[256,256]{1,0:T(8,128)(2,1)S(1)}, bf16[256,256]{1,0:T(8,128)(2,1)S(1)}, u32[]{:S(2)}, u32[]{:S(2)}) collective-permute-start(bf16[256,256]{1,0:T(8,128)(2,1)S(1)} %get-tuple-element.173), channel_id=1, source_target_pairs={{0,3},{1,2},{2,1},{3,0},{4,7},{5,6},{6,5},{7,4},{8,11},{9,10},{10,... | collective-permute-start | bytes 393224 | tf_op jit(solution)/shard_map/ppermute | solution.py:144
  482.7 62.7 %collective-permute-start.67 = (bf16[256,256]{1,0:T(8,128)(2,1)S(1)}, bf16[256,256]{1,0:T(8,128)(2,1)S(1)}, u32[]{:S(2)}, u32[]{:S(2)}) collective-permute-start(bf16[256,256]{1,0:T(8,128)(2,1)S(1)} %get-tuple-element.174), channel_id=1, source_target_pairs={{0,2},{1,3},{2,0},{3,1},{4,6},{5,7},{6,4},{7,5},{8,10},{9,11},{10,... | collective-permute-start | bytes 393224 | tf_op jit(solution)/shard_map/ppermute | solution.py:144
  483.1 62.3 %collective-permute-start.66 = (bf16[256,256]{1,0:T(8,128)(2,1)S(1)}, bf16[256,256]{1,0:T(8,128)(2,1)S(1)}, u32[]{:S(2)}, u32[]{:S(2)}) collective-permute-start(bf16[256,256]{1,0:T(8,128)(2,1)S(1)} %get-tuple-element.175), channel_id=1, source_target_pairs={{0,1},{1,0},{2,3},{3,2},{4,5},{5,4},{6,7},{7,6},{8,9},{9,8},{10,11... | collective-permute-start | bytes 393224 | tf_op jit(solution)/shard_map/ppermute | solution.py:144
  546.4 89.4 %all-gather.16.cloned.1.call-start = ((), (), s32[]{:S(2)}) async-start(), calls=%async_computation.11 | async-start | bytes 1310720 | tf_op jit(solution)/shard_map/all_gather | solution.py:341
  552.9 96.3 %all-gather.18.cloned.1.call-start = ((), (), s32[]{:S(2)}) async-start(), calls=%async_computation.12 | async-start | bytes 1310720 | tf_op jit(solution)/shard_map/all_gather | solution.py:341
  566.8 152.8 %reduce-scatter.5.cloned.1.call-start = ((), (), s32[]{:S(2)}) async-start(), calls=%async_computation.6 | async-start | bytes 1990656 | tf_op jit(solution)/shard_map/reduce_scatter | solution.py:339
  584.7 43.8 %collective-permute-start.65 = (bf16[256,1024]{1,0:T(8,128)(2,1)}, bf16[256,1024]{1,0:T(8,128)(2,1)}, u32[]{:S(2)}, u32[]{:S(2)}) collective-permute-start(bf16[256,1024]{1,0:T(8,128)(2,1)} %fusion.44), channel_id=1, source_target_pairs={{0,2},{1,3},{2,0},{3,1},{4,6},{5,7},{6,4},{7,5},{8,10},{9,11},{10,... | collective-permute-start | bytes 1572872 | tf_op jit(solution)/shard_map/ppermute | solution.py:144
  588.7 41.8 %collective-permute-start.45 = (bf16[256,1024]{1,0:T(8,128)(2,1)}, bf16[256,1024]{1,0:T(8,128)(2,1)}, u32[]{:S(2)}, u32[]{:S(2)}) collective-permute-start(bf16[256,1024]{1,0:T(8,128)(2,1)} %fusion.58), channel_id=1, source_target_pairs={{0,2},{1,3},{2,0},{3,1},{4,6},{5,7},{6,4},{7,5},{8,10},{9,11},{10,... | collective-permute-start | bytes 1572872 | tf_op jit(solution)/shard_map/ppermute | solution.py:144
  591.3 41.1 %collective-permute-start.55 = (bf16[256,1024]{1,0:T(8,128)(2,1)}, bf16[256,1024]{1,0:T(8,128)(2,1)}, u32[]{:S(2)}, u32[]{:S(2)}) collective-permute-start(bf16[256,1024]{1,0:T(8,128)(2,1)} %fusion.51), channel_id=1, source_target_pairs={{0,2},{1,3},{2,0},{3,1},{4,6},{5,7},{6,4},{7,5},{8,10},{9,11},{10,... | collective-permute-start | bytes 1572872 | tf_op jit(solution)/shard_map/ppermute | solution.py:144
  (170 other events, 2694.4 us)
Sparse Core Ops, SparseCore 0:
  19.3 51.7 all-gather.13
  73.1 50.3 all-gather.9
  154.7 48.9 all-gather.11
  378.3 68.5 reduce-scatter.8
  457.4 68.4 reduce-scatter.10
  546.6 62.8 reduce-scatter.6
  611.1 18.7 all-gather.15
  631.5 17.6 all-gather.17
  653.0 66.5 reduce-scatter.4

commit v2 on v1

--- a/solution.py
+++ b/solution.py
@@ -157,6 +157,18 @@
         other = swap((exact(2) + got[rows:].astype(F32)).astype(BF16), 2)
         return exact(0) + got[:rows].astype(F32) + other.astype(F32)
 
+    def halve(array, order):
+        me = lax.axis_index("fsdp")
+        width = n.bit_length() - 1
+        array = array.reshape((2,) * width + array.shape[1:])
+        for bit in order:
+            mine = (me >> bit) & 1
+            part = lambda side: lax.dynamic_index_in_dim(array, side, width - 1 - bit)
+            pairs = [(i, i ^ (1 << bit)) for i in range(n)]
+            got = lax.ppermute(part(1 - mine), "fsdp", pairs)
+            array = (part(mine).astype(F32) + got.astype(F32)).astype(BF16)
+        return array.reshape(array.shape[width:])
+
     def exchange(blocks):
         me = lax.axis_index("seq")
         return [blocks(me)] + [swap(blocks(me ^ d), d) for d in range(1, k)]
@@ -207,13 +219,16 @@
         )
         count = small.shape[0]
         extra = 16
-        small = jnp.pad(small, (0, extra * 3 * wide - count)).reshape(extra, 3 * wide)
+        small = jnp.pad(small, (0, extra * D - count)).reshape(extra, D)
         mine = lax.dynamic_index_in_dim(
             qkv_weight.reshape(shard, 3, k, wide), me, 2, keepdims=False
         ).reshape(shard, 3 * wide)
+        out_mine = lax.dynamic_slice_in_dim(out_weight, me * wide, wide, 1)
+        mine = jnp.concatenate([mine, out_mine], axis=1)
         packed = lax.all_gather(jnp.concatenate([mine, small], axis=0), "fsdp", axis=0)
-        w_qkv = packed[:, :shard].reshape(D, 3 * wide)
-        vectors = packed[:, shard:].reshape(n, extra * 3 * wide)[:, :count].astype(F32)
+        w_qkv = packed[:, :shard, : 3 * wide].reshape(D, 3 * wide)
+        out_columns = packed[:, :shard, 3 * wide :].reshape(D, wide)
+        vectors = packed[:, shard:].reshape(n, extra * D)[:, :count].astype(F32)
         vector = lambda j: vectors[:, j * shard : (j + 1) * shard].reshape(1, D)
         (qbias, vbias, obias, gain_one, shift_one, dbias, gain_two, shift_two) = [
             vector(j) for j in range(8)
@@ -229,8 +244,6 @@
             [jnp.full((1, wide), DH ** (-0.5), F32), jnp.ones((1, 2 * wide), F32)], axis=1
         )
 
-        out_mine = lax.dynamic_slice_in_dim(out_weight, me * wide, wide, 1)
-        out_columns = lax.all_gather(out_mine, "fsdp", axis=0, tiled=True)
         w_out = jnp.concatenate(
             absolute(exchange(lambda t: lax.dynamic_slice_in_dim(out_columns, t * wide, wide, 0))),
             axis=1,
@@ -289,11 +302,12 @@
             grad_hidden = grad_two + scatter(dot(grad_pre, w_up, NT))
             grads.append(grad_hidden)
 
-        def shared(grad):
-            return lax.psum_scatter(grad.astype(BF16), "fsdp", scatter_dimension=0, tiled=True)
-
-        r_down = shared(g_down)
-        r_up = shared(g_up)
+        r_hidden = lax.psum_scatter(
+            jnp.concatenate([g_up.astype(BF16), g_down.astype(BF16)], axis=1),
+            "fsdp",
+            scatter_dimension=0,
+            tiled=True,
+        )
 
         for i in range(seqs):
             x, seg_col, seg_row, qkv, context, lse = state[i][:6]
@@ -313,11 +327,9 @@
             grad_tokens.append(grad_one + scatter(dot(dqkv, w_qkv, NT)))
 
         g_out = g_out.astype(BF16)
-        r_out = shared(
-            jnp.concatenate(
-                absolute(exchange(lambda t: lax.dynamic_slice_in_dim(g_out, t * wide, wide, 1))),
-                axis=0,
-            )
+        out_rows = jnp.concatenate(
+            absolute(exchange(lambda t: lax.dynamic_slice_in_dim(g_out, t * wide, wide, 1))),
+            axis=0,
         )
 
         place = lambda v: lax.dynamic_update_slice_in_dim(
@@ -328,34 +340,42 @@
             jnp.zeros((n, k, unit_shard), F32), s_pre.reshape(n, 1, unit_shard), me, 1
         ).reshape(n, k * unit_shard)
         vector_sums = jnp.concatenate([v.reshape(n, shard) for v in full] + [hidden_sum], axis=1)
-        vector_sums = jnp.pad(vector_sums, ((0, 0), (0, extra * 3 * wide - count)))
+        vector_sums = jnp.pad(vector_sums, ((0, 0), (0, extra * D - count)))
         joined = jnp.concatenate(
             [
-                g_qkv.astype(BF16).reshape(n, shard, 3 * wide),
-                vector_sums.astype(BF16).reshape(n, extra, 3 * wide),
+                jnp.concatenate([g_qkv.astype(BF16), out_rows], axis=1).reshape(n, shard, D),
+                vector_sums.astype(BF16).reshape(n, extra, D),
             ],
             axis=1,
         )
-        r_qkv = lax.psum_scatter(joined, "fsdp", scatter_dimension=0, tiled=True)[0]
-
         every = lambda a: lax.all_gather(a, "seq", axis=0)
-        all_down = every(r_down).reshape(k * unit_shard, D).astype(F32)
+        both, joined = lax.optimization_barrier((every(r_hidden), joined))
+        bits = list(range(n.bit_length() - 1))
+        r_qkv = jnp.concatenate(
+            [
+                halve(joined[..., : D // 2], bits),
+                halve(joined[..., D // 2 :], bits[1:] + bits[:1]),
+            ],
+            axis=1,
+        )
+
         all_up = (
-            every(r_up)
+            both[..., :units]
             .reshape(k, shard, n, unit_shard)
             .transpose(1, 2, 0, 3)
             .reshape(shard, FF)
             .astype(F32)
         )
-        all_out = every(r_out).transpose(1, 0, 2).reshape(shard, D).astype(F32)
+        all_down = both[..., units:].reshape(k * unit_shard, D).astype(F32)
         last = every(r_qkv)
         all_qkv = (
-            last[:, :shard]
+            last[:, :shard, : 3 * wide]
             .reshape(k, shard, 3, wide)
             .transpose(1, 2, 0, 3)
             .reshape(shard, 3 * D)
             .astype(F32)
         )
+        all_out = last[:, :shard, 3 * wide :].transpose(1, 0, 2).reshape(shard, D).astype(F32)
         vec = jnp.sum(last[:, shard:].astype(F32), axis=0).reshape(-1)[:count]
         piece = lambda j: vec[j * shard : (j + 1) * shard]
         return (

time: 745 us -> 695 us (0.933)
  blocking collectives: 60.1 us -> 0 us
  waiting for transfers between devices: 295 us -> 259 us
  other arithmetic: 57.3 us -> 73 us
  matrix products: 124 us -> 138 us
  local copies, waits for them, and re-layouts: 47 us -> 59 us
    reduce_scatter x4 -> x0, waiting for transfers between devices: 84.2 us -> none  [the longest x1 67.6 us: body(): r_qkv = lax.psum_scatter(joined, 'fsdp', scatter_dimension=0, tiled=True)[0]]
    all_gather x3 -> x0, blocking collectives: 60.1 us -> none  [the longest x1 32.9 us: body(): out_columns = lax.all_gather(out_mine, 'fsdp', axis=0, tiled=True)]
    ppermute x0 -> x6, waiting for transfers between devices: none -> 27.1 us  [halve(): got = lax.ppermute(part(1 - mine), 'fsdp', pairs)]
    all_gather x1, waiting for transfers between devices: 0.01 us -> 24.2 us  [body(): lax.all_gather(jnp.concatenate([mine, small], axis=0), 'fsdp', axis=0)]
    concatenate x2 -> x4, other arithmetic: 2.2 us -> 15.8 us  [the longest x1 10.7 us: body(): jnp.concatenate([g_qkv.astype(BF16), out_rows], axis=1).reshape(n, shard, D)]
    dot_general x36, matrix products: 124 us -> 138 us  [dot(): return lax.dot_general(a, b, dims, preferred_element_type=F32)]
    ppermute x0 -> x6, starting transfers between devices: none -> 8.31 us  [halve(): got = lax.ppermute(part(1 - mine), 'fsdp', pairs)]
    unnamed x252 -> x233, local copies, waits for them, and re-layouts: 27.1 us -> 33.4 us
  transfers between devices with their start and end apart: 78 -> 81, of which waited for: 27 -> 30; matrix products, arithmetic and copies ran while one was open for 24% -> 31% of each run, Pallas kernels for 12% -> 13%
where the time goes in v2:
time: 695 us; the launch traced here: 687 us
  waiting for transfers between devices  259 us (37%)
  matrix products  138 us (20%)
  Pallas kernels  89.8 us (13%)
  other arithmetic  73 us (11%)
  local copies, waits for them, and re-layouts  59 us (8%)
  starting transfers between devices  51.9 us (7%)
  between operations  16.9 us (2%)
    ppermute x69, waiting for transfers between devices, swap(): return lax.ppermute(array, 'seq', [(i, i ^ flip) for i in range(k)])  202 us
    dot_general x36, matrix products, dot(): return lax.dot_general(a, b, dims, preferred_element_type=F32)  138 us
    pallas_call x3, Pallas kernels, attend_back(): pl.pallas_call(back_kernel, grid=(length // QBLK,), in_specs=[pl.BlockSpe...  51.4 us
    ppermute x69, starting transfers between devices, swap(): return lax.ppermute(array, 'seq', [(i, i ^ flip) for i in range(k)])  43.3 us
    pallas_call x3, Pallas kernels, attend(): pl.pallas_call(attend_kernel, grid=(length // QBLK,), in_specs=[pl.BlockS...  38.4 us
    unnamed x233, local copies, waits for them, and re-layouts  33.4 us
    ppermute x6, waiting for transfers between devices, halve(): got = lax.ppermute(part(1 - mine), 'fsdp', pairs)  27.1 us
    all_gather x1, waiting for transfers between devices, body(): lax.all_gather(jnp.concatenate([mine, small], axis=0), 'fsdp', axis=0)  24.2 us
  transfers between devices with their start and end apart: 81, of which 30 were waited for; matrix products, arithmetic and copies ran while one was open for 31% of the time, Pallas kernels for 13%

profile of v2, /device:TPU:0, one launch (start us, length us, event | category | flops | bytes accessed | tf_op | source)
XLA Modules:
  0.0 687.0 jit_solution(6406781966706467482)
XLA Ops:
  32.1 18.8 %collective-permute-done.17 = bf16[256,1024]{1,0:T(8,128)(2,1)} collective-permute-done((bf16[256,1024]{1,0:T(8,128)(2,1)}, bf16[256,1024]{1,0:T(8,128)(2,1)}, u32[]{:S(2)}, u32[]{:S(2)}) %collective-permute-start.17) | collective-permute-done | bytes 524320 | tf_op jit(solution)/shard_map/ppermute | solution.py:144
  50.9 24.2 %all-gather.13.cloned.1.call-done = bf16[1152,1024]{1,0:T(8,128)(2,1)} async-done(((bf16[144,1024]{1,0:T(8,128)(2,1)}), bf16[1152,1024]{1,0:T(8,128)(2,1)}) %all-gather.13.cloned.1.call-update) | async-done | bytes 2359312 | tf_op jit(solution)/shard_map/all_gather | solution.py:228
  89.1 12.8 %shard_map.272 = (bf16[1024,256]{1,0:T(8,128)(2,1)S(1)}, f32[4,1024]{1,0:T(4,128)S(1)}) custom-call(bf16[1024,768]{1,0:T(8,128)(2,1)S(1)} %multiply_convert_fusion.7.q_ref.k_ref.v_ref, bf16[1024,768]{1,0:T(8,128)(2,1)S(1)} %multiply_convert_fusion.7.q_ref.k_ref.v_ref, bf16[1024,768]{1,0:T(8,128)(2,1)S(1)} %multiply_convert_fusion.7.q_ref.k_ref.v_ref, ...), custom_call_target="tpu_custom_call" | custom-call | flops 4294967296 | bytes 2097152 | tf_op jit(solution)/shard_map/pallas_call | solution.py:43
  102.0 12.6 %shard_map.273 = (bf16[1024,256]{1,0:T(8,128)(2,1)S(1)}, f32[4,1024]{1,0:T(4,128)S(1)}) custom-call(bf16[1024,768]{1,0:T(8,128)(2,1)S(1)} %multiply_convert_fusion.6.q_ref.k_ref.v_ref, bf16[1024,768]{1,0:T(8,128)(2,1)S(1)} %multiply_convert_fusion.6.q_ref.k_ref.v_ref, bf16[1024,768]{1,0:T(8,128)(2,1)S(1)} %multiply_convert_fusion.6.q_ref.k_ref.v_ref, ...), custom_call_target="tpu_custom_call" | custom-call | flops 4294967296 | bytes 2097152 | tf_op jit(solution)/shard_map/pallas_call | solution.py:43
  118.2 12.9 %shard_map.271 = (bf16[1024,256]{1,0:T(8,128)(2,1)S(1)}, f32[4,1024]{1,0:T(4,128)S(1)}) custom-call(bf16[1024,768]{1,0:T(8,128)(2,1)S(1)} %multiply_convert_fusion.8.q_ref.k_ref.v_ref, bf16[1024,768]{1,0:T(8,128)(2,1)S(1)} %multiply_convert_fusion.8.q_ref.k_ref.v_ref, bf16[1024,768]{1,0:T(8,128)(2,1)S(1)} %multiply_convert_fusion.8.q_ref.k_ref.v_ref, ...), custom_call_target="tpu_custom_call" | custom-call | flops 4294967296 | bytes 2097152 | tf_op jit(solution)/shard_map/pallas_call | solution.py:43
  151.6 11.2 %collective-permute-done.30 = bf16[256,1024]{1,0:T(8,128)(2,1)} collective-permute-done((bf16[256,1024]{1,0:T(8,128)(2,1)}, bf16[256,1024]{1,0:T(8,128)(2,1)}, u32[]{:S(2)}, u32[]{:S(2)}) %collective-permute-start.30) | collective-permute-done | bytes 524320 | tf_op jit(solution)/shard_map/ppermute | solution.py:144
  162.8 10.7 %collective-permute-done.20 = bf16[256,1024]{1,0:T(8,128)(2,1)} collective-permute-done((bf16[256,1024]{1,0:T(8,128)(2,1)}, bf16[256,1024]{1,0:T(8,128)(2,1)}, u32[]{:S(2)}, u32[]{:S(2)}) %collective-permute-start.20) | collective-permute-done | bytes 524320 | tf_op jit(solution)/shard_map/ppermute | solution.py:144
  182.5 13.1 %collective-permute-done.22 = bf16[256,1024]{1,0:T(8,128)(2,1)} collective-permute-done((bf16[256,1024]{1,0:T(8,128)(2,1)}, bf16[256,1024]{1,0:T(8,128)(2,1)}, u32[]{:S(2)}, u32[]{:S(2)}) %collective-permute-start.22) | collective-permute-done | bytes 524320 | tf_op jit(solution)/shard_map/ppermute | solution.py:144
  196.2 9.2 %collective-permute-done.12 = bf16[256,1024]{1,0:T(8,128)(2,1)} collective-permute-done((bf16[256,1024]{1,0:T(8,128)(2,1)}, bf16[256,1024]{1,0:T(8,128)(2,1)}, u32[]{:S(2)}, u32[]{:S(2)}) %collective-permute-start.12) | collective-permute-done | bytes 524320 | tf_op jit(solution)/shard_map/ppermute | solution.py:144
  233.6 11.1 %collective-permute-done.15 = bf16[256,1024]{1,0:T(8,128)(2,1)S(1)} collective-permute-done((bf16[256,1024]{1,0:T(8,128)(2,1)S(1)}, bf16[256,1024]{1,0:T(8,128)(2,1)S(1)}, u32[]{:S(2)}, u32[]{:S(2)}) %collective-permute-start.15) | collective-permute-done | bytes 524320 | tf_op jit(solution)/shard_map/ppermute | solution.py:144
  244.7 10.3 %collective-permute-done.25 = bf16[256,1024]{1,0:T(8,128)(2,1)S(1)} collective-permute-done((bf16[256,1024]{1,0:T(8,128)(2,1)S(1)}, bf16[256,1024]{1,0:T(8,128)(2,1)S(1)}, u32[]{:S(2)}, u32[]{:S(2)}) %collective-permute-start.25) | collective-permute-done | bytes 524320 | tf_op jit(solution)/shard_map/ppermute | solution.py:144
  257.5 11.8 %collective-permute-done.32 = bf16[256,1024]{1,0:T(8,128)(2,1)S(1)} collective-permute-done((bf16[256,1024]{1,0:T(8,128)(2,1)S(1)}, bf16[256,1024]{1,0:T(8,128)(2,1)S(1)}, u32[]{:S(2)}, u32[]{:S(2)}) %collective-permute-start.32) | collective-permute-done | bytes 524320 | tf_op jit(solution)/shard_map/ppermute | solution.py:144
  284.6 12.5 %collective-permute-done.35 = bf16[256,1024]{1,0:T(8,128)(2,1)S(1)} collective-permute-done((bf16[256,1024]{1,0:T(8,128)(2,1)S(1)}, bf16[256,1024]{1,0:T(8,128)(2,1)S(1)}, u32[]{:S(2)}, u32[]{:S(2)}) %collective-permute-start.35) | collective-permute-done | bytes 524320 | tf_op jit(solution)/shard_map/ppermute | solution.py:144
  306.0 12.0 %collective-permute-done.57 = bf16[256,1024]{1,0:T(8,128)(2,1)} collective-permute-done((bf16[256,1024]{1,0:T(8,128)(2,1)}, bf16[256,1024]{1,0:T(8,128)(2,1)}, u32[]{:S(2)}, u32[]{:S(2)}) %collective-permute-start.57) | collective-permute-done | bytes 524320 | tf_op jit(solution)/shard_map/ppermute | solution.py:144
  329.7 9.0 %collective-permute-done.47 = bf16[256,1024]{1,0:T(8,128)(2,1)} collective-permute-done((bf16[256,1024]{1,0:T(8,128)(2,1)}, bf16[256,1024]{1,0:T(8,128)(2,1)}, u32[]{:S(2)}, u32[]{:S(2)}) %collective-permute-start.47) | collective-permute-done | bytes 524320 | tf_op jit(solution)/shard_map/ppermute | solution.py:144
  404.0 11.1 %collective-permute-done.60 = bf16[256,1024]{1,0:T(8,128)(2,1)S(1)} collective-permute-done((bf16[256,1024]{1,0:T(8,128)(2,1)S(1)}, bf16[256,1024]{1,0:T(8,128)(2,1)S(1)}, u32[]{:S(2)}, u32[]{:S(2)}) %collective-permute-start.60) | collective-permute-done | bytes 524320 | tf_op jit(solution)/shard_map/ppermute | solution.py:144
  417.0 9.2 %collective-permute-done.40 = bf16[256,1024]{1,0:T(8,128)(2,1)S(1)} collective-permute-done((bf16[256,1024]{1,0:T(8,128)(2,1)S(1)}, bf16[256,1024]{1,0:T(8,128)(2,1)S(1)}, u32[]{:S(2)}, u32[]{:S(2)}) %collective-permute-start.40) | collective-permute-done | bytes 524320 | tf_op jit(solution)/shard_map/ppermute | solution.py:144
  428.2 8.9 %collective-permute-done.50 = bf16[256,1024]{1,0:T(8,128)(2,1)S(1)} collective-permute-done((bf16[256,1024]{1,0:T(8,128)(2,1)S(1)}, bf16[256,1024]{1,0:T(8,128)(2,1)S(1)}, u32[]{:S(2)}, u32[]{:S(2)}) %collective-permute-start.50) | collective-permute-done | bytes 524320 | tf_op jit(solution)/shard_map/ppermute | solution.py:144
  448.3 9.0 %collective-permute-done.62 = bf16[256,1024]{1,0:T(8,128)(2,1)} collective-permute-done((bf16[256,1024]{1,0:T(8,128)(2,1)}, bf16[256,1024]{1,0:T(8,128)(2,1)}, u32[]{:S(2)}, u32[]{:S(2)}) %collective-permute-start.62) | collective-permute-done | bytes 524320 | tf_op jit(solution)/shard_map/ppermute | solution.py:144
  469.9 8.6 %collective-permute-done.42 = bf16[256,1024]{1,0:T(8,128)(2,1)} collective-permute-done((bf16[256,1024]{1,0:T(8,128)(2,1)}, bf16[256,1024]{1,0:T(8,128)(2,1)}, u32[]{:S(2)}, u32[]{:S(2)}) %collective-permute-start.42) | collective-permute-done | bytes 524320 | tf_op jit(solution)/shard_map/ppermute | solution.py:144
  490.3 17.3 %shard_map.274 = bf16[1024,768]{1,0:T(8,128)(2,1)S(1)} custom-call(bf16[1024,768]{1,0:T(8,128)(2,1)S(1)} %copy-done.22, bf16[1024,768]{1,0:T(8,128)(2,1)S(1)} %copy-done.22, bf16[1024,768]{1,0:T(8,128)(2,1)S(1)} %copy-done.22, bf16[1024,256]{1,0:T(8,128)(2,1)S(1)} %convolution_convert_fusion.2.do_ref, f32[4,1024]{1,0:T(4,128)S(1)} %get-tuple-element.26.lse_ref, ...), custom_call_target="tpu_custom_call" | custom-call | flops 10737418240 | bytes 3670016 | tf_op jit(solution)/shard_map/pallas_call | solution.py:104
  510.5 17.0 %shard_map.276 = bf16[1024,768]{1,0:T(8,128)(2,1)S(1)} custom-call(bf16[1024,768]{1,0:T(8,128)(2,1)S(1)} %copy-done.20, bf16[1024,768]{1,0:T(8,128)(2,1)S(1)} %copy-done.20, bf16[1024,768]{1,0:T(8,128)(2,1)S(1)} %copy-done.20, bf16[1024,256]{1,0:T(8,128)(2,1)S(1)} %convolution_convert_fusion.do_ref, f32[4,1024]{1,0:T(4,128)S(1)} %get-tuple-element.28.lse_ref, ...), custom_call_target="tpu_custom_call" | custom-call | flops 10737418240 | bytes 3670016 | tf_op jit(solution)/shard_map/pallas_call | solution.py:104
  529.9 17.1 %shard_map.275 = bf16[1024,768]{1,0:T(8,128)(2,1)S(1)} custom-call(bf16[1024,768]{1,0:T(8,128)(2,1)S(1)} %copy-done.18, bf16[1024,768]{1,0:T(8,128)(2,1)S(1)} %copy-done.18, bf16[1024,768]{1,0:T(8,128)(2,1)S(1)} %copy-done.18, bf16[1024,256]{1,0:T(8,128)(2,1)S(1)} %convolution_convert_fusion.1.do_ref, f32[4,1024]{1,0:T(4,128)S(1)} %get-tuple-element.27.lse_ref, ...), custom_call_target="tpu_custom_call" | custom-call | flops 10737418240 | bytes 3670016 | tf_op jit(solution)/shard_map/pallas_call | solution.py:104
  583.4 10.7 %maximum_maximum_fusion = bf16[1024,1024]{0,1:T(8,128)(2,1)S(1)} fusion(bf16[256,256]{0,1:T(8,128)(2,1)S(1)} %bitcast.300, bf16[256,256]{0,1:T(8,128)(2,1)S(1)} %bitcast.301, bf16[256,256]{0,1:T(8,128)(2,1)S(1)} %bitcast.302, bf16[256,256]{0,1:T(8,128)(2,1)S(1)} %bitcast.299, bf16[1024,768]{0,1:T(8,128)(2,1)} %add_convert_fusion.2), kind=kLoop, calls=%fused_computation.55 | loop fusion | flops 10485760 | bytes 4194304 | tf_op jit(solution)/shard_map/concatenate | solution.py:346
  (590 shorter events, 368.9 us)
Async XLA Ops:
  7.2 67.9 %all-gather.13.cloned.1.call-start = ((), (), s32[]{:S(2)}) async-start(), calls=%async_computation.3 | async-start | bytes 2654208 | tf_op jit(solution)/shard_map/all_gather | solution.py:228
  20.2 185.2 %all-gather.9.cloned.1.call-start = ((), (), s32[]{:S(2)}) async-start(), calls=%async_computation.1 | async-start | bytes 2359296 | tf_op jit(solution)/shard_map/all_gather | solution.py:254
  24.6 55.0 %collective-permute-start.1 = (bf16[256,1024]{1,0:T(8,128)(2,1)}, bf16[256,1024]{1,0:T(8,128)(2,1)}, u32[]{:S(2)}, u32[]{:S(2)}) collective-permute-start(bf16[256,1024]{1,0:T(8,128)(2,1)} %get-tuple-element.170), channel_id=1, source_target_pairs={{0,2},{1,3},{2,0},{3,1},{4,6},{5,7},{6,4},{7,5},{8,10},{9,11},{10,... | collective-permute-start | bytes 1572872 | tf_op jit(solution)/shard_map/ppermute | solution.py:144
  26.5 88.1 %collective-permute-start = (bf16[256,1024]{1,0:T(8,128)(2,1)}, bf16[256,1024]{1,0:T(8,128)(2,1)}, u32[]{:S(2)}, u32[]{:S(2)}) collective-permute-start(bf16[256,1024]{1,0:T(8,128)(2,1)} %get-tuple-element.170), channel_id=1, source_target_pairs={{0,1},{1,0},{2,3},{3,2},{4,5},{5,4},{6,7},{7,6},{8,9},{9,8},{10,11... | collective-permute-start | bytes 1572872 | tf_op jit(solution)/shard_map/ppermute | solution.py:144
  28.9 190.9 %all-gather.11.cloned.1.call-start = ((), (), s32[]{:S(2)}) async-start(), calls=%async_computation.2 | async-start | bytes 2359296 | tf_op jit(solution)/shard_map/all_gather | solution.py:256
  29.3 50.9 %collective-permute-start.16 = (bf16[256,1024]{1,0:T(8,128)(2,1)}, bf16[256,1024]{1,0:T(8,128)(2,1)}, u32[]{:S(2)}, u32[]{:S(2)}) collective-permute-start(bf16[256,1024]{1,0:T(8,128)(2,1)} %get-tuple-element.172), channel_id=1, source_target_pairs={{0,1},{1,0},{2,3},{3,2},{4,5},{5,4},{6,7},{7,6},{8,9},{9,8},{10,11... | collective-permute-start | bytes 1572872 | tf_op jit(solution)/shard_map/ppermute | solution.py:144
  29.7 50.0 %collective-permute-start.27 = (bf16[256,1024]{1,0:T(8,128)(2,1)S(1)}, bf16[256,1024]{1,0:T(8,128)(2,1)}, u32[]{:S(2)}, u32[]{:S(2)}) collective-permute-start(bf16[256,1024]{1,0:T(8,128)(2,1)S(1)} %get-tuple-element.171), channel_id=1, source_target_pairs={{0,2},{1,3},{2,0},{3,1},{4,6},{5,7},{6,4},{7,5},{8,10},{9,11},{10,... | collective-permute-start | bytes 1572872 | tf_op jit(solution)/shard_map/ppermute | solution.py:144
  79.7 34.9 %collective-permute-start.2 = (bf16[256,1024]{1,0:T(8,128)(2,1)}, bf16[256,1024]{1,0:T(8,128)(2,1)S(1)}, u32[]{:S(2)}, u32[]{:S(2)}) collective-permute-start(bf16[256,1024]{1,0:T(8,128)(2,1)} %collective-permute-done.1), channel_id=1, source_target_pairs={{0,1},{1,0},{2,3},{3,2},{4,5},{5,4},{6,7},{7,6},{8,9},{9,8},{10,11... | collective-permute-start | bytes 1572872 | tf_op jit(solution)/shard_map/ppermute | solution.py:144
  80.3 50.8 %collective-permute-start.8 = (bf16[256,256]{1,0:T(8,128)(2,1)S(1)}, bf16[256,256]{1,0:T(8,128)(2,1)S(1)}, u32[]{:S(2)}, u32[]{:S(2)}) collective-permute-start(bf16[256,256]{1,0:T(8,128)(2,1)S(1)} %get-tuple-element.189), channel_id=1, source_target_pairs={{0,3},{1,2},{2,1},{3,0},{4,7},{5,6},{6,5},{7,4},{8,11},{9,10},{10,... | collective-permute-start | bytes 393224 | tf_op jit(solution)/shard_map/ppermute | solution.py:144
  85.3 45.8 %collective-permute-start.7 = (bf16[256,256]{1,0:T(8,128)(2,1)S(1)}, bf16[256,256]{1,0:T(8,128)(2,1)S(1)}, u32[]{:S(2)}, u32[]{:S(2)}) collective-permute-start(bf16[256,256]{1,0:T(8,128)(2,1)S(1)} %get-tuple-element.190), channel_id=1, source_target_pairs={{0,2},{1,3},{2,0},{3,1},{4,6},{5,7},{6,4},{7,5},{8,10},{9,11},{10,... | collective-permute-start | bytes 393224 | tf_op jit(solution)/shard_map/ppermute | solution.py:144
  85.8 45.3 %collective-permute-start.6 = (bf16[256,256]{1,0:T(8,128)(2,1)S(1)}, bf16[256,256]{1,0:T(8,128)(2,1)S(1)}, u32[]{:S(2)}, u32[]{:S(2)}) collective-permute-start(bf16[256,256]{1,0:T(8,128)(2,1)S(1)} %get-tuple-element.191), channel_id=1, source_target_pairs={{0,1},{1,0},{2,3},{3,2},{4,5},{5,4},{6,7},{7,6},{8,9},{9,8},{10,11... | collective-permute-start | bytes 393224 | tf_op jit(solution)/shard_map/ppermute | solution.py:144
  143.2 421.5 %reduce-scatter.4.cloned.1.call-start = ((), (), s32[]{:S(2)}) async-start(), calls=%async_computation.6 | async-start | bytes 4718592
  348.6 51.5 %collective-permute-start.59 = (bf16[512,1024]{1,0:T(8,128)(2,1)S(1)}, bf16[512,1024]{1,0:T(8,128)(2,1)S(1)}, u32[]{:S(2)}, u32[]{:S(2)}) collective-permute-start(bf16[512,1024]{1,0:T(8,128)(2,1)S(1)} %pad_maximum_fusion.26), channel_id=1, source_target_pairs={{0,1},{1,0},{2,3},{3,2},{4,5},{5,4},{6,7},{7,6},{8,9},{9,8},{10,11... | collective-permute-start | bytes 3145736 | tf_op jit(solution)/shard_map/ppermute | solution.py:144
  359.2 42.3 %collective-permute-start.39 = (bf16[512,1024]{1,0:T(8,128)(2,1)S(1)}, bf16[512,1024]{1,0:T(8,128)(2,1)S(1)}, u32[]{:S(2)}, u32[]{:S(2)}) collective-permute-start(bf16[512,1024]{1,0:T(8,128)(2,1)S(1)} %pad_maximum_fusion.22), channel_id=1, source_target_pairs={{0,1},{1,0},{2,3},{3,2},{4,5},{5,4},{6,7},{7,6},{8,9},{9,8},{10,11... | collective-permute-start | bytes 3145736 | tf_op jit(solution)/shard_map/ppermute | solution.py:144
  402.7 34.4 %collective-permute-start.50 = (bf16[256,1024]{1,0:T(8,128)(2,1)S(1)}, bf16[256,1024]{1,0:T(8,128)(2,1)S(1)}, u32[]{:S(2)}, u32[]{:S(2)}) collective-permute-start(bf16[256,1024]{1,0:T(8,128)(2,1)S(1)} %fusion.55), channel_id=1, source_target_pairs={{0,2},{1,3},{2,0},{3,1},{4,6},{5,7},{6,4},{7,5},{8,10},{9,11},{10,... | collective-permute-start | bytes 1572872 | tf_op jit(solution)/shard_map/ppermute | solution.py:144
  466.3 138.1 %all-gather.15.cloned.1.call-start = ((), (), s32[]{:S(2)}) async-start(), calls=%async_computation.4 | async-start | bytes 2621440 | tf_op jit(solution)/shard_map/all_gather | solution.py:351
  486.3 95.2 %collective-permute-start.68 = (bf16[256,256]{1,0:T(8,128)(2,1)}, bf16[256,256]{1,0:T(8,128)(2,1)}, u32[]{:S(2)}, u32[]{:S(2)}) collective-permute-start(bf16[256,256]{1,0:T(8,128)(2,1)} %get-tuple-element.181), channel_id=1, source_target_pairs={{0,3},{1,2},{2,1},{3,0},{4,7},{5,6},{6,5},{7,4},{8,11},{9,10},{10,... | collective-permute-start | bytes 393224 | tf_op jit(solution)/shard_map/ppermute | solution.py:144
  487.1 94.7 %collective-permute-start.67 = (bf16[256,256]{1,0:T(8,128)(2,1)}, bf16[256,256]{1,0:T(8,128)(2,1)}, u32[]{:S(2)}, u32[]{:S(2)}) collective-permute-start(bf16[256,256]{1,0:T(8,128)(2,1)} %get-tuple-element.182), channel_id=1, source_target_pairs={{0,2},{1,3},{2,0},{3,1},{4,6},{5,7},{6,4},{7,5},{8,10},{9,11},{10,... | collective-permute-start | bytes 393224 | tf_op jit(solution)/shard_map/ppermute | solution.py:144
  487.9 93.8 %collective-permute-start.66 = (bf16[256,256]{1,0:T(8,128)(2,1)}, bf16[256,256]{1,0:T(8,128)(2,1)}, u32[]{:S(2)}, u32[]{:S(2)}) collective-permute-start(bf16[256,256]{1,0:T(8,128)(2,1)} %get-tuple-element.183), channel_id=1, source_target_pairs={{0,1},{1,0},{2,3},{3,2},{4,5},{5,4},{6,7},{7,6},{8,9},{9,8},{10,11... | collective-permute-start | bytes 393224 | tf_op jit(solution)/shard_map/ppermute | solution.py:144
  554.1 44.4 %collective-permute-start.64 = (bf16[512,1024]{1,0:T(8,128)(2,1)}, bf16[512,1024]{1,0:T(8,128)(2,1)}, u32[]{:S(2)}, u32[]{:S(2)}) collective-permute-start(bf16[512,1024]{1,0:T(8,128)(2,1)} %pad_maximum_fusion.27), channel_id=1, source_target_pairs={{0,1},{1,0},{2,3},{3,2},{4,5},{5,4},{6,7},{7,6},{8,9},{9,8},{10,11... | collective-permute-start | bytes 3145736 | tf_op jit(solution)/shard_map/ppermute | solution.py:144
  559.4 42.8 %collective-permute-start.44 = (bf16[512,1024]{1,0:T(8,128)(2,1)}, bf16[512,1024]{1,0:T(8,128)(2,1)}, u32[]{:S(2)}, u32[]{:S(2)}) collective-permute-start(bf16[512,1024]{1,0:T(8,128)(2,1)} %pad_maximum_fusion.23), channel_id=1, source_target_pairs={{0,1},{1,0},{2,3},{3,2},{4,5},{5,4},{6,7},{7,6},{8,9},{9,8},{10,11... | collective-permute-start | bytes 3145736 | tf_op jit(solution)/shard_map/ppermute | solution.py:144
  566.8 102.7 %all-gather.17.cloned.1.call-start = ((), (), s32[]{:S(2)}) async-start(), calls=%async_computation.5 | async-start | bytes 1474560 | tf_op jit(solution)/shard_map/all_gather | solution.py:351
  603.7 48.9 %collective-permute-start.45 = (bf16[256,1024]{1,0:T(8,128)(2,1)S(1)}, bf16[256,1024]{1,0:T(8,128)(2,1)}, u32[]{:S(2)}, u32[]{:S(2)}) collective-permute-start(bf16[256,1024]{1,0:T(8,128)(2,1)S(1)} %fusion.58), channel_id=1, source_target_pairs={{0,2},{1,3},{2,0},{3,1},{4,6},{5,7},{6,4},{7,5},{8,10},{9,11},{10,... | collective-permute-start | bytes 1572872 | tf_op jit(solution)/shard_map/ppermute | solution.py:144
  610.9 43.6 %collective-permute-start.55 = (bf16[256,1024]{1,0:T(8,128)(2,1)S(1)}, bf16[256,1024]{1,0:T(8,128)(2,1)}, u32[]{:S(2)}, u32[]{:S(2)}) collective-permute-start(bf16[256,1024]{1,0:T(8,128)(2,1)S(1)} %fusion.51), channel_id=1, source_target_pairs={{0,2},{1,3},{2,0},{3,1},{4,6},{5,7},{6,4},{7,5},{8,10},{9,11},{10,... | collective-permute-start | bytes 1572872 | tf_op jit(solution)/shard_map/ppermute | solution.py:144
  (162 other events, 2224.9 us)
Sparse Core Ops, SparseCore 0:
  20.3 54.7 all-gather.12
  77.2 49.6 all-gather.8
  143.3 46.8 all-gather.10
  466.4 86.4 reduce-scatter.3
  566.9 21.0 all-gather.14
  652.7 16.7 all-gather.16
